TPU v7x, 32 devices: a whole 2x2x4 slice. The times are simulated.
32 devices in a mesh: chan: 2 (over y), tile: 16 (over z, x, core).
Axes of the slice: x: 2, y: 2, z: 4, core: 2. Of those that a mesh axis runs over, the one named last changes fastest.
Arguments:
- image: bfloat16 [256, 256, 256], P('chan', 'tile'), may hold values from -6 to 6
- w_down: bfloat16 [2, 2, 256, 512], P(None, None, None, 'chan'), may hold values from -0.1875 to 0.1875
- w_mix: bfloat16 [3, 3, 512, 512], P(None, None, None, 'chan'), may hold values from -0.09375 to 0.09375
- cotangent: bfloat16 [512, 128, 128], P('chan', 'tile'), may hold values from -6 to 6
Outputs:
- mixed: bfloat16 [512, 128, 128], P('chan', 'tile')
- grad_mix: float32 [512, 3, 3, 512], P('tile', None, None, 'chan')
- grad_down: float32 [256, 2, 2, 512], P('tile', None, None, 'chan')
- grad_image: bfloat16 [256, 256, 256], P('chan', 'tile')
All inputs are finite; a program needn't handle non-finite values.
Results may differ from a plain program's by a relative error of at most 0.0049.
Values may be sent and summed in bfloat16 or wider, within the bound.
A program may use at most 64 MiB of HBM per device.

v0:
```python
import math

import jax
import jax.numpy as jnp
from jax import lax
from jax.sharding import PartitionSpec as P


def with_halo(block, sides, width):
    for axis, dim in sides:
        count = lax.axis_size(axis)
        forward = [(i, i + 1) for i in range(count - 1)]
        backward = [(target, source) for source, target in forward]
        low = lax.ppermute(
            lax.slice_in_dim(block, block.shape[dim] - width, None, axis=dim), axis, forward
        )
        high = lax.ppermute(lax.slice_in_dim(block, 0, width, axis=dim), axis, backward)
        block = jnp.concatenate([low, block, high], axis=dim)
    return block


def normal_cdf(value):
    return 0.5 * (1.0 + jax.scipy.special.erf(value / math.sqrt(2.0)))


def normal_pdf(value):
    return jnp.exp(-0.5 * value * value) / math.sqrt(2.0 * math.pi)


def per_device(image, w_down, w_mix, cotangent):
    n_tile = lax.axis_size("tile")
    own_out = cotangent.shape[0]
    n_rows = cotangent.shape[1]
    n_cols = cotangent.shape[2]
    own_in = image.shape[0]
    scale = 1.0 / math.sqrt(n_rows * n_tile * n_cols)
    wide_image = lax.all_gather(image, "chan", axis=0, tiled=True)
    in_chan = wide_image.shape[0]
    patches = wide_image.reshape(in_chan, n_rows, 2, n_cols, 2)
    preact = jnp.einsum("crawb,abcd->drw", patches, w_down, preferred_element_type=jnp.float32)
    hidden = (preact * normal_cdf(preact)).astype(jnp.bfloat16)
    plain = lax.all_gather(hidden, "chan", axis=0, tiled=True)
    full_hidden = with_halo(plain, (("tile", 1),), 1)
    hidden_pad = jnp.pad(full_hidden, ((0, 0), (0, 0), (1, 1)))
    all_chan = hidden_pad.shape[0]
    mixed_sum = jnp.zeros((own_out, n_rows, n_cols), jnp.float32)
    for tap_row in range(3):
        for tap_col in range(3):
            window = hidden_pad[:, tap_row : tap_row + n_rows, tap_col : tap_col + n_cols]
            mixed_sum = mixed_sum + jnp.einsum(
                "crw,cd->drw", window, w_mix[tap_row, tap_col], preferred_element_type=jnp.float32
            )
    mixed = mixed_sum.astype(jnp.bfloat16)
    cot_rimmed = with_halo(cotangent, (("tile", 1),), 1)
    part = hidden_pad
    terms = []
    for tap_row in range(3):
        for tap_col in range(3):
            window = part[:, tap_row : tap_row + n_rows, tap_col : tap_col + n_cols]
            terms.append(
                jnp.einsum("crw,drw->cd", window, cotangent, preferred_element_type=jnp.float32)
            )
    grad_mix = (
        lax.psum_scatter(
            jnp.stack(terms, 1).reshape(all_chan // n_tile * lax.axis_size("tile"), 3, 3, own_out),
            "tile",
            scatter_dimension=0,
            tiled=True,
        )
        * scale
    )
    cot_pad = jnp.pad(cot_rimmed, ((0, 0), (0, 0), (1, 1)))
    total = jnp.zeros((own_out * lax.axis_size("chan"), n_rows, n_cols), jnp.float32)
    for tap_row in range(3):
        for tap_col in range(3):
            back = cot_pad[
                :, 2 - tap_row : 2 - tap_row + n_rows, 2 - tap_col : 2 - tap_col + n_cols
            ]
            filters = w_mix[tap_row, tap_col]
            total = total + jnp.einsum(
                "drw,cd->crw", back, filters, preferred_element_type=jnp.float32
            )
    grad_hidden = lax.psum_scatter(total, "chan", scatter_dimension=0, tiled=True)
    slope = normal_cdf(preact) + preact * normal_pdf(preact)
    grad_pre = (grad_hidden * slope).astype(jnp.bfloat16)
    part = patches
    grad_down = (
        lax.psum_scatter(
            jnp.einsum("crawb,drw->cabd", part, grad_pre, preferred_element_type=jnp.float32),
            "tile",
            scatter_dimension=0,
            tiled=True,
        )
        * scale
    )
    down_turned = lax.all_to_all(w_down, "chan", split_axis=2, concat_axis=3, tiled=True)
    filters = down_turned
    term = jnp.einsum(
        "drw,abcd->crawb",
        lax.all_gather(grad_pre, "chan", axis=0, tiled=True),
        filters,
        preferred_element_type=jnp.float32,
    )
    grad_image = term.reshape(jnp.zeros((own_in, 2 * n_rows, 2 * n_cols), jnp.float32).shape)
    return (mixed, grad_mix, grad_down, grad_image.astype(jnp.bfloat16))


def solution(mesh):
    return jax.shard_map(
        per_device,
        mesh=mesh,
        in_specs=(
            P("chan", "tile", None),
            P(None, None, None, "chan"),
            P(None, None, None, "chan"),
            P("chan", "tile", None),
        ),
        out_specs=(
            P("chan", "tile", None),
            P("tile", None, None, "chan"),
            P("tile", None, None, "chan"),
            P("chan", "tile", None),
        ),
        check_vma=False,
    )
```

profile of v0, /device:TPU:0, one launch (start us, length us, event | category | flops | bytes accessed | tf_op | source)
XLA Modules:
  0.0 316.2 jit_solution(12937387532468863622)
XLA Ops:
  7.2 1.5 copy.109
  8.7 2.4 collective-permute-start.2
  11.1 1.3 collective-permute-start.3
  12.9 3.4 %collective-permute-done.3 = bf16[256,1,128]{0,2,1:T(8,128)(2,1)S(1)} collective-permute-done((bf16[256,1,128]{0,2,1:T(8,128)(2,1)S(1)}, bf16[256,1,128]{0,2,1:T(8,128)(2,1)S(1)}, u32[]{:S(2)}, u32[]{:S(2)}) %collective-permute-start.3) | collective-permute-done | bytes 65568 | tf_op jit(solution)/shard_map/ppermute | solution.py:17
  19.9 2.6 bitcast_add_fusion
  22.5 27.8 %all-gather.4.cloned.1.call-done = bf16[256,16,256]{2,1,0:T(8,128)(2,1)} async-done(((bf16[128,16,256]{2,1,0:T(8,128)(2,1)}), bf16[256,16,256]{2,1,0:T(8,128)(2,1)}) %all-gather.4.cloned.1.call-update) | async-done | bytes 2097168 | tf_op jit(solution)/shard_map/all_gather | solution.py:37
  50.3 3.0 copy.88
  53.3 2.2 reshape.16
  55.5 3.3 %fusion.11 = f32[256,8,128]{2,0,1:T(8,128)} fusion(bf16[256,8,2,128,2]{0,4,3,2,1:T(2,128)(2,1)} %reshape.16, bf16[2,2,256,256]{3,2,1,0:T(8,128)(2,1)S(1)} %copy-done.10), kind=kOutput, calls=%fused_computation.22 | convolution fusion | flops 536870912 | bytes 3670016 | tf_op jit(solution)/shard_map/crawb,abcd->drw/dot_general | solution.py:40
  58.9 25.5 %reduce-scatter.5.cloned.1.call-done = f32[256,8,128]{2,0,1:T(8,128)} async-done(((f32[512,8,128]{2,0,1:T(8,128)}), f32[256,8,128]{2,0,1:T(8,128)}) %reduce-scatter.5.cloned.1.call-update) | async-done | bytes 1048592 | tf_op jit(solution)/shard_map/reduce_scatter | solution.py:83
  84.4 2.9 fusion.40
  87.3 1.7 fusion.14
  89.0 2.2 copy.124
  91.3 17.4 %all-gather.6.cloned.1.call-done = bf16[512,8,128]{2,0,1:T(8,128)(2,1)} async-done(((bf16[256,8,128]{2,0,1:T(8,128)(2,1)}), bf16[512,8,128]{2,0,1:T(8,128)(2,1)}) %all-gather.6.cloned.1.call-update) | async-done | bytes 1048592 | tf_op jit(solution)/shard_map/all_gather | solution.py:42
  109.7 1.7 collective-permute-start
  113.0 2.9 collective-permute-done.1
  116.0 2.8 fusion.5
  124.4 2.1 copy-done.5
  127.5 1.3 copy.125
  128.9 3.7 %all-to-all-start = ((bf16[2,2,256,256]{3,1,0,2:T(2,128)(2,1)}), bf16[2,2,256,256]{3,1,0,2:T(2,128)(2,1)S(1)}, u32[]{:S(2)}, u32[]{:S(2)}) async-start(bf16[2,2,256,256]{3,1,0,2:T(2,128)(2,1)} %copy.125), calls=%async_computation.2 | async-start | bytes 1048576 | tf_op jit(solution)/shard_map/all_to_all | solution.py:96
  133.8 5.3 %all-to-all-done = bf16[2,2,256,256]{3,1,0,2:T(2,128)(2,1)S(1)} async-done(((bf16[2,2,256,256]{3,1,0,2:T(2,128)(2,1)}), bf16[2,2,256,256]{3,1,0,2:T(2,128)(2,1)S(1)}, u32[]{:S(2)}, u32[]{:S(2)}) %all-to-all-start) | async-done | bytes 524320 | tf_op jit(solution)/shard_map/all_to_all | solution.py:96
  139.1 1.3 copy.166
  140.4 1.4 reshape.41
  141.8 63.9 %all-reduce.5.cloned.1.call-done = f32[256,2,2,256]{3,2,1,0:T(2,128)} async-done(((f32[256,2,2,256]{3,2,1,0:T(2,128)}), f32[256,2,2,256]{3,2,1,0:T(2,128)}) %all-reduce.5.cloned.1.call-update) | async-done | bytes 1048592
  205.7 1.5 dynamic-slice_multiply_fusion
  207.2 20.6 %all-gather.8.cloned.1.call-done = bf16[512,8,128]{2,0,1:T(8,128)(2,1)} async-done(((bf16[256,8,128]{2,0,1:T(8,128)(2,1)}), bf16[512,8,128]{2,0,1:T(8,128)(2,1)}) %all-gather.8.cloned.1.call-update) | async-done | bytes 1048592 | tf_op jit(solution)/shard_map/all_gather | solution.py:100
  227.8 2.0 fusion.17
  229.8 2.1 copy.128
  231.9 2.6 copy.130
  234.6 1.9 fusion.95
  243.1 64.5 %reduce-scatter.3.cloned.1.call-done = f32[32,3,3,256]{3,0,2,1:T(8,128)} async-done(((f32[512,3,3,256]{3,0,2,1:T(8,128)}), f32[32,3,3,256]{3,0,2,1:T(8,128)}) %reduce-scatter.3.cloned.1.call-update) | async-done | bytes 294928 | tf_op jit(solution)/shard_map/reduce_scatter | solution.py:64
  307.6 1.7 broadcast_multiply_fusion
  (73 shorter events, 20.5 us)
Async XLA Ops:
  7.2 5.3 %copy-start.1 = (bf16[3,3,512,256]{3,2,1,0:T(8,128)(2,1)S(1)}, bf16[3,3,512,256]{3,2,1,0:T(8,128)(2,1)}, u32[]{:S(2)}) copy-start(bf16[3,3,512,256]{3,2,1,0:T(8,128)(2,1)} %param.6) | copy-start | bytes 7077892
  7.2 43.1 %all-gather.4.cloned.1.call-start = ((), (), s32[]{:S(2)}) async-start(), calls=%async_computation.3 | async-start | bytes 3145728 | tf_op jit(solution)/shard_map/all_gather | solution.py:37
  8.7 4.2 %collective-permute-start.2 = (bf16[256,1,128]{0,2,1:T(8,128)(2,1)S(1)}, bf16[256,1,128]{0,2,1:T(8,128)(2,1)S(1)}, u32[]{:S(2)}, u32[]{:S(2)}) collective-permute-start(bf16[256,1,128]{0,2,1:T(8,128)(2,1)S(1)} %get-tuple-element.23), channel_id=1, source_target_pairs={{0,1},{1,2},{2,3},{3,4},{4,5},{5,6},{6,7},{7,8},{8,9},{9,10},{10,1... | collective-permute-start | bytes 196616 | tf_op jit(solution)/shard_map/ppermute | solution.py:14
  11.1 5.3 %collective-permute-start.3 = (bf16[256,1,128]{0,2,1:T(8,128)(2,1)S(1)}, bf16[256,1,128]{0,2,1:T(8,128)(2,1)S(1)}, u32[]{:S(2)}, u32[]{:S(2)}) collective-permute-start(bf16[256,1,128]{0,2,1:T(8,128)(2,1)S(1)} %get-tuple-element.22), channel_id=1, source_target_pairs={{1,0},{2,1},{3,2},{4,3},{5,4},{6,5},{7,6},{8,7},{9,8},{10,9},{11,1... | collective-permute-start | bytes 196616 | tf_op jit(solution)/shard_map/ppermute | solution.py:17
  12.4 72.0 %reduce-scatter.5.cloned.1.call-start = ((), (), s32[]{:S(2)}) async-start(), calls=%async_computation.6 | async-start | bytes 3145728 | tf_op jit(solution)/shard_map/reduce_scatter | solution.py:83
  22.5 86.2 %all-gather.6.cloned.1.call-start = ((), (), s32[]{:S(2)}) async-start(), calls=%async_computation.4 | async-start | bytes 1572864 | tf_op jit(solution)/shard_map/all_gather | solution.py:42
  53.3 2.2 copy-start.10
  58.9 28.5 %copy-start.8 = (bf16[256,8,2,128,2]{0,4,3,2,1:T(2,128)(2,1)S(1)}, bf16[256,8,2,128,2]{0,4,3,2,1:T(2,128)(2,1)}, u32[]{:S(2)}) copy-start(bf16[256,8,2,128,2]{0,4,3,2,1:T(2,128)(2,1)} %reshape.16) | copy-start | bytes 6291460
  87.2 1.8 copy-start.9
  87.3 118.5 %all-reduce.5.cloned.1.call-start = ((), (), s32[]{:S(2)}) async-start(), calls=%async_computation.8 | async-start | bytes 2097152
  91.3 136.5 %all-gather.8.cloned.1.call-start = ((), (), s32[]{:S(2)}) async-start(), calls=%async_computation.7 | async-start | bytes 1572864 | tf_op jit(solution)/shard_map/all_gather | solution.py:100
  109.7 3.3 %collective-permute-start = (bf16[512,1,128]{2,0,1:T(8,128)(2,1)S(1)}, bf16[512,1,128]{2,0,1:T(8,128)(2,1)S(1)}, u32[]{:S(2)}, u32[]{:S(2)}) collective-permute-start(bf16[512,1,128]{2,0,1:T(8,128)(2,1)S(1)} %get-tuple-element.20), channel_id=1, source_target_pairs={{0,1},{1,2},{2,3},{3,4},{4,5},{5,6},{6,7},{7,8},{8,9},{9,10},{10,1... | collective-permute-start | bytes 393224 | tf_op jit(solution)/shard_map/ppermute | solution.py:14
  111.5 4.5 %collective-permute-start.1 = (bf16[512,1,128]{2,0,1:T(8,128)(2,1)S(1)}, bf16[512,1,128]{2,0,1:T(8,128)(2,1)S(1)}, u32[]{:S(2)}, u32[]{:S(2)}) collective-permute-start(bf16[512,1,128]{2,0,1:T(8,128)(2,1)S(1)} %get-tuple-element.21), channel_id=1, source_target_pairs={{1,0},{2,1},{3,2},{4,3},{5,4},{6,5},{7,6},{8,7},{9,8},{10,9},{11,1... | collective-permute-start | bytes 393224 | tf_op jit(solution)/shard_map/ppermute | solution.py:17
  112.8 194.8 %reduce-scatter.3.cloned.1.call-start = ((), (), s32[]{:S(2)}) async-start(), calls=%async_computation.5 | async-start | bytes 5013504 | tf_op jit(solution)/shard_map/reduce_scatter | solution.py:64
  118.8 1.2 copy-start
  120.4 1.5 copy-start.6
  122.3 1.0 copy-start.3
  124.3 2.2 copy-start.5
  126.5 1.0 copy-start.11
  126.5 6.1 %copy-start.12 = (u32[32]{0:T(128)S(1)}, u32[32]{0:T(128)}, u32[]{:S(2)}) copy-start(u32[32]{0:T(128)} %constant.25) | copy-start | bytes 388
  128.9 10.2 %all-to-all-start = ((bf16[2,2,256,256]{3,1,0,2:T(2,128)(2,1)}), bf16[2,2,256,256]{3,1,0,2:T(2,128)(2,1)S(1)}, u32[]{:S(2)}, u32[]{:S(2)}) async-start(bf16[2,2,256,256]{3,1,0,2:T(2,128)(2,1)} %copy.125), calls=%async_computation.2 | async-start | bytes 1048576 | tf_op jit(solution)/shard_map/all_to_all | solution.py:96
  234.6 2.1 copy-start.2
  237.9 1.3 copy-start.7
  238.8 1.4 copy-start.4
Sparse Core Ops, SparseCore 0:
  12.5 37.7 all-gather.3
  52.5 31.8 reduce-scatter.4
  87.4 21.2 all-gather.5
  112.4 93.2 all-reduce.4
  207.2 20.5 all-gather.7
  232.0 75.5 reduce-scatter.2
where the time goes:
time: 317 us; the launch traced here: 316 us
  waiting for transfers between devices  231 us (73%)
  local copies, waits for them, and re-layouts  25.4 us (8%)
  matrix products  24.4 us (8%)
  between operations  15.2 us (5%)
  starting transfers between devices  10.8 us (3%)
  other arithmetic  9.06 us (3%)
    reduce_scatter x1, waiting for transfers between devices, per_device(): lax.psum_scatter(jnp.stack(terms, 1).reshape(all_chan // n_tile * lax.axi...  64.5 us
    unnamed x7, waiting for transfers between devices  64 us
    all_gather x1, waiting for transfers between devices, per_device(): wide_image = lax.all_gather(image, 'chan', axis=0, tiled=True)  27.8 us
    reduce_scatter x1, waiting for transfers between devices, per_device(): lax.psum_scatter(total, 'chan', scatter_dimension=0, tiled=True)  25.5 us
    all_gather x1, waiting for transfers between devices, per_device(): lax.all_gather(grad_pre, 'chan', axis=0, tiled=True)  20.6 us
    all_gather x1, waiting for transfers between devices, per_device(): plain = lax.all_gather(hidden, 'chan', axis=0, tiled=True)  17.4 us
    unnamed x32, local copies, waits for them, and re-layouts  11.7 us
    dot_general x9, matrix products, per_device(): jnp.einsum('crw,cd->drw', window, w_mix[tap_row, tap_col], preferred_elem...  6.81 us
  transfers between devices with their start and end apart: 11, of which 9 were waited for; matrix products, arithmetic and copies ran while one was open for 15% of the time, Pallas kernels for 0%

commit v1 on v0

--- a/solution.py
+++ b/solution.py
@@ -105,9 +105,142 @@
     return (mixed, grad_mix, grad_down, grad_image.astype(jnp.bfloat16))
 
 
+def flip(block, axis, mask):
+    count = lax.axis_size(axis)
+    return lax.ppermute(block, axis, [(i, i ^ mask) for i in range(count)])
+
+
+def tap_sum(padded, weights, n_rows, n_cols, back):
+    total = None
+    for i in range(3):
+        for j in range(3):
+            r, c = (2 - i, 2 - j) if back else (i, j)
+            window = padded[:, r : r + n_rows, c : c + n_cols]
+            form = "drw,cd->crw" if back else "crw,cd->drw"
+            term = jnp.einsum(form, window, weights[i, j], preferred_element_type=jnp.float32)
+            total = term if total is None else total + term
+    return total
+
+
+def halve(block, dim, bit):
+    mine = (lax.axis_index("tile") >> bit) & 1
+    keep = lax.dynamic_index_in_dim(block, mine, dim, keepdims=False)
+    send = lax.dynamic_index_in_dim(block, 1 - mine, dim, keepdims=False)
+    got = flip(send.astype(jnp.bfloat16), "tile", 1 << bit)
+    return keep.astype(jnp.float32) + got.astype(jnp.float32)
+
+
+def reduce_halves(own, other, top):
+    taps, half, depth = own.shape
+    share = half >> top
+    own_bits = list(range(top))
+    other_bits = own_bits[:1] + own_bits[:0:-1]
+    sums = []
+    for block, order in ((own, own_bits), (other, other_bits)):
+        left = list(range(top))[::-1]
+        block = block.reshape((taps,) + (2,) * top + (share, depth))
+        for bit in order:
+            block = halve(block, 1 + left.index(bit), bit)
+            left.remove(bit)
+        sums.append(block)
+    here = (lax.axis_index("tile") >> top) == lax.axis_index("chan")
+    keep = jnp.where(here, sums[0], sums[1])
+    send = jnp.where(here, sums[1], sums[0])
+    return keep + flip(send.astype(jnp.bfloat16), "tile", 1 << top).astype(jnp.float32)
+
+
+def edge_rows(block, cross):
+    n_tile = lax.axis_size("tile")
+    down, up = [], []
+    for k in range(2):
+        to = (1 - k if cross else k) * n_tile
+        for i in range(n_tile - 1):
+            down.append((k * n_tile + i, to + i + 1))
+            up.append((k * n_tile + i + 1, to + i))
+    low = lax.ppermute(block[:, -1:], ("chan", "tile"), down)
+    high = lax.ppermute(block[:, :1], ("chan", "tile"), up)
+    return low, high
+
+
+def rimmed(block, edges):
+    low, high = edges
+    return jnp.pad(jnp.concatenate([low, block, high], axis=1), ((0, 0), (0, 0), (1, 1)))
+
+
+def pair_device(image, w_down, w_mix, cotangent):
+    bf16, f32 = jnp.bfloat16, jnp.float32
+    n_tile = lax.axis_size("tile")
+    top = n_tile.bit_length() - 2
+    own_out, n_rows, n_cols = cotangent.shape
+    own_in = image.shape[0]
+    scale = 1.0 / math.sqrt(n_rows * n_tile * n_cols)
+    k = lax.axis_index("chan")
+
+    def part(weights, which, dim, size):
+        return lax.dynamic_slice_in_dim(weights, which * size, size, dim)
+
+    image_far = flip(image, "chan", 1)
+    cot_edges = edge_rows(cotangent, False)
+    down_own, down_far = part(w_down, k, 2, own_in), part(w_down, 1 - k, 2, own_in)
+    mix_own, mix_far = part(w_mix, k, 2, own_out), part(w_mix, 1 - k, 2, own_out)
+    down_back = flip(down_far, "chan", 1)
+
+    cot_pad = rimmed(cotangent, cot_edges)
+    away = tap_sum(cot_pad, mix_far, n_rows, n_cols, True)
+    got = flip(away.astype(bf16), "chan", 1)
+    grad_hidden = tap_sum(cot_pad, mix_own, n_rows, n_cols, True)
+
+    def taps_of(block):
+        return block.reshape(own_in, n_rows, 2, n_cols, 2)
+
+    near, far = taps_of(image), taps_of(image_far)
+    preact = jnp.einsum("crawb,abcd->drw", near, down_own, preferred_element_type=f32)
+    preact = preact + jnp.einsum("crawb,abcd->drw", far, down_far, preferred_element_type=f32)
+    cdf = normal_cdf(preact)
+    hidden = (preact * cdf).astype(bf16)
+    hidden_far = flip(hidden, "chan", 1)
+    own_edges, far_edges = edge_rows(hidden, False), edge_rows(hidden, True)
+
+    slope = cdf + preact * normal_pdf(preact)
+    grad_pre = ((grad_hidden + got.astype(f32)) * slope).astype(bf16)
+    grad_pre_far = flip(grad_pre, "chan", 1)
+
+    def mix_terms(padded):
+        terms = []
+        for i in range(3):
+            for j in range(3):
+                window = padded[:, i : i + n_rows, j : j + n_cols]
+                terms.append(
+                    jnp.einsum("crw,drw->cd", window, cotangent, preferred_element_type=f32)
+                )
+        return jnp.stack(terms)
+
+    own_pad = rimmed(hidden, own_edges)
+    far_pad = rimmed(hidden_far, far_edges)
+    grad_mix = reduce_halves(mix_terms(own_pad), mix_terms(far_pad), top) * scale
+    grad_mix = grad_mix.transpose(1, 0, 2).reshape(-1, 3, 3, own_out)
+    mixed = tap_sum(own_pad, mix_own, n_rows, n_cols, False)
+    mixed = (mixed + tap_sum(far_pad, mix_far, n_rows, n_cols, False)).astype(bf16)
+
+    def down_terms(patches):
+        term = jnp.einsum("crawb,drw->abcd", patches, grad_pre, preferred_element_type=f32)
+        return term.reshape(4, own_in, own_out)
+
+    grad_down = reduce_halves(down_terms(near), down_terms(far), top) * scale
+    grad_down = grad_down.transpose(1, 0, 2).reshape(-1, 2, 2, own_out)
+    term = jnp.einsum("drw,abcd->crawb", grad_pre, down_own, preferred_element_type=f32)
+    term = term + jnp.einsum(
+        "drw,abcd->crawb", grad_pre_far, down_back, preferred_element_type=f32
+    )
+    return (mixed, grad_mix, grad_down, term.astype(bf16).reshape(image.shape))
+
+
 def solution(mesh):
+    sizes = dict(mesh.shape)
+    n_tile = sizes["tile"]
+    paired = sizes["chan"] == 2 and n_tile > 1 and n_tile & (n_tile - 1) == 0
     return jax.shard_map(
-        per_device,
+        pair_device if paired else per_device,
         mesh=mesh,
         in_specs=(
             P("chan", "tile", None),

time: 317 us -> 133 us (0.42)
  waiting for transfers between devices: 231 us -> 38.3 us
  starting transfers between devices: 10.8 us -> 46 us
  between operations: 15.2 us -> 1.6 us
  local copies, waits for them, and re-layouts: 25.4 us -> 11.9 us
  matrix products: 24.4 us -> 30.7 us
  other arithmetic: 9.06 us -> 4.49 us
    reduce_scatter x2 -> x0, waiting for transfers between devices: 90 us -> none  [the longest x1 64.5 us: per_device(): lax.psum_scatter(jnp.stack(terms, 1).reshape(all_chan // n_tile * lax.axi...]
    all_gather x3 -> x0, waiting for transfers between devices: 65.7 us -> none  [the longest x1 27.8 us: per_device(): wide_image = lax.all_gather(image, 'chan', axis=0, tiled=True)]
    unnamed x7 -> x0, waiting for transfers between devices: 64 us -> none
    ppermute x4 -> x25, starting transfers between devices: 6.69 us -> 46 us  [the longest x19 35.8 us: flip(): return lax.ppermute(block, axis, [(i, i ^ mask) for i in range(count)])]
    ppermute x4 -> x25, waiting for transfers between devices: 6.32 us -> 38.3 us  [the longest x19 37.8 us: flip(): return lax.ppermute(block, axis, [(i, i ^ mask) for i in range(count)])]
    dot_general x30 -> x60, matrix products: 24.4 us -> 30.7 us  [the longest x36 15.7 us: tap_sum(): jnp.einsum(form, window, weights[i, j], preferred_element_type=jnp.float32)]
    all_to_all x1 -> x0, waiting for transfers between devices: 5.26 us -> none  [per_device(): lax.all_to_all(w_down, 'chan', split_axis=2, concat_axis=3, tiled=True)]
    all_to_all x1 -> x0, starting transfers between devices: 3.71 us -> none  [per_device(): lax.all_to_all(w_down, 'chan', split_axis=2, concat_axis=3, tiled=True)]
  transfers between devices with their start and end apart: 11 -> 25, of which waited for: 9 -> 9; matrix products, arithmetic and copies ran while one was open for 15% -> 32% of each run, Pallas kernels for 0% -> 0%
where the time goes in v1:
time: 133 us
  starting transfers between devices  46 us (35%)
  waiting for transfers between devices  38.3 us (29%)
  matrix products  30.7 us (23%)
  local copies, waits for them, and re-layouts  11.9 us (9%)
  other arithmetic  4.49 us (3%)
  between operations  1.6 us (1%)
    ppermute x19, waiting for transfers between devices, flip(): return lax.ppermute(block, axis, [(i, i ^ mask) for i in range(count)])  37.8 us
    ppermute x19, starting transfers between devices, flip(): return lax.ppermute(block, axis, [(i, i ^ mask) for i in range(count)])  35.8 us
    dot_general x36, matrix products, tap_sum(): jnp.einsum(form, window, weights[i, j], preferred_element_type=jnp.float32)  15.7 us
    unnamed x38, local copies, waits for them, and re-layouts  8.27 us
    dot_general x18, matrix products, mix_terms(): jnp.einsum('crw,drw->cd', window, cotangent, preferred_element_type=f32)  6.47 us
    ppermute x3, starting transfers between devices, edge_rows(): low = lax.ppermute(block[:, -1:], ('chan', 'tile'), down)  6.09 us
    ppermute x3, starting transfers between devices, edge_rows(): high = lax.ppermute(block[:, :1], ('chan', 'tile'), up)  4.03 us
  transfers between devices with their start and end apart: 25, of which 9 were waited for; matrix products, arithmetic and copies ran while one was open for 32% of the time, Pallas kernels for 0%

profile of v1, /device:TPU:0, one launch (start us, length us, event | category | flops | bytes accessed | tf_op | source)
XLA Modules:
  0.0 133.0 jit_solution(2026892365443944662)
XLA Ops:
  0.7 1.3 copy.150
  2.6 1.3 collective-permute-start.14
  3.9 3.0 %collective-permute-start.13 = (bf16[256,1,128]{2,0,1:T(8,128)(2,1)}, bf16[256,1,128]{2,0,1:T(8,128)(2,1)S(1)}, u32[]{:S(2)}, u32[]{:S(2)}) collective-permute-start(bf16[256,1,128]{2,0,1:T(8,128)(2,1)} %get-tuple-element.12), channel_id=1, source_target_pairs={{0,1},{1,2},{2,3},{3,4},{4,5},{5,6},{6,7},{7,8},{8,9},{9,10},{10,1... | collective-permute-start | bytes 196616 | tf_op jit(solution)/shard_map/ppermute | solution.py:160
  6.9 2.7 %copy.126 = bf16[128,16,256]{0,2,1:T(8,128)(2,1)} copy(bf16[128,16,256]{2,1,0:T(8,128)(2,1)} %param.4) | data formatting | bytes 2097152 | tf_op args[0]
  9.6 3.0 %collective-permute-start = (bf16[128,16,256]{0,2,1:T(8,128)(2,1)}, bf16[128,16,256]{0,2,1:T(8,128)(2,1)}, u32[]{:S(2)}, u32[]{:S(2)}) collective-permute-start(bf16[128,16,256]{0,2,1:T(8,128)(2,1)} %copy.126), channel_id=1, source_target_pairs={{0,16},{16,0},{1,17},{17,1},{2,18},{18,2},{3,19},{19,3},{4,20},{20... | collective-permute-start | bytes 3145736 | tf_op jit(solution)/shard_map/ppermute | solution.py:110
  13.3 2.6 %convolution_bitcast_fusion.1 = f32[256,8,128]{0,2,1:T(8,128)} fusion(bf16[128,8,2,128,2]{0,4,3,2,1:T(2,128)(2,1)} %bitcast.358, bf16[2,2,256,256]{3,2,1,0:T(8,128)(2,1)S(1)} %copy-done.6, s32[]{:T(128)S(6)} %select_n.81), kind=kOutput, calls=%fused_computation.48 | convolution fusion | flops 268435456 | bytes 2359300 | tf_op jit(solution)/shard_map/crawb,abcd->drw/dot_general | solution.py:197
  20.8 2.0 %collective-permute-start.15 = (bf16[256,8,128]{0,2,1:T(8,128)(2,1)S(1)}, bf16[256,8,128]{0,2,1:T(8,128)(2,1)S(1)}, u32[]{:S(2)}, u32[]{:S(2)}) collective-permute-start(bf16[256,8,128]{0,2,1:T(8,128)(2,1)S(1)} %fusion.18), channel_id=1, source_target_pairs={{0,16},{16,0},{1,17},{17,1},{2,18},{18,2},{3,19},{19,3},{4,20},{20... | collective-permute-start | bytes 1572872 | tf_op jit(solution)/shard_map/ppermute | solution.py:110
  26.6 9.7 %collective-permute-done = bf16[128,16,256]{0,2,1:T(8,128)(2,1)} collective-permute-done((bf16[128,16,256]{0,2,1:T(8,128)(2,1)}, bf16[128,16,256]{0,2,1:T(8,128)(2,1)}, u32[]{:S(2)}, u32[]{:S(2)}) %collective-permute-start) | collective-permute-done | bytes 1048608 | tf_op jit(solution)/shard_map/ppermute | solution.py:110
  36.3 1.8 %multiply_convert_fusion = (bf16[256,8,128]{0,2,1:T(8,128)(2,1)S(1)}, f32[256,8,128]{0,2,1:T(8,128)S(1)}) fusion(f32[256,8,128]{0,2,1:T(8,128)S(1)} %copy-done.3, bf16[128,8,2,128,2]{0,4,3,2,1:T(2,128)(2,1)} %bitcast.9, bf16[2,2,128,256]{3,2,1,0:T(8,128)(2,1)} %constant_dynamic-slice_fusion.4), kind=kOutput, calls=%fused_computation.70 | convolution fusion | flops 270008320 | bytes 3932160 | tf_op jit(solution)/shard_map/crawb,abcd->drw/dot_general | solution.py:198
  38.1 14.9 %collective-permute-done.15 = bf16[256,8,128]{0,2,1:T(8,128)(2,1)S(1)} collective-permute-done((bf16[256,8,128]{0,2,1:T(8,128)(2,1)S(1)}, bf16[256,8,128]{0,2,1:T(8,128)(2,1)S(1)}, u32[]{:S(2)}, u32[]{:S(2)}) %collective-permute-start.15) | collective-permute-done | bytes 524320 | tf_op jit(solution)/shard_map/ppermute | solution.py:110
  54.3 2.5 %collective-permute-start.24 = (bf16[256,8,128]{0,2,1:T(8,128)(2,1)S(1)}, bf16[256,8,128]{0,2,1:T(8,128)(2,1)S(1)}, u32[]{:S(2)}, u32[]{:S(2)}) collective-permute-start(bf16[256,8,128]{0,2,1:T(8,128)(2,1)S(1)} %fusion.17), channel_id=1, source_target_pairs={{0,16},{16,0},{1,17},{17,1},{2,18},{18,2},{3,19},{19,3},{4,20},{20... | collective-permute-start | bytes 1572872 | tf_op jit(solution)/shard_map/ppermute | solution.py:110
  56.8 1.8 %fusion.27 = f32[256,128,2,2,1]{0,1,4,3,2:T(8,128)S(1)} fusion(bf16[128,8,2,128,2]{0,4,3,2,1:T(2,128)(2,1)} %bitcast.9, bf16[256,8,128]{0,2,1:T(8,128)(2,1)S(1)} %fusion.17), kind=kOutput, calls=%fused_computation.66 | convolution fusion | flops 268435456 | bytes 2097152 | tf_op jit(solution)/shard_map/crawb,drw->abcd/dot_general | solution.py:226
  59.6 1.7 %collective-permute-start.1 = (bf16[256,1,128]{0,2,1:T(8,128)(2,1)S(1)}, bf16[256,1,128]{0,2,1:T(8,128)(2,1)S(1)}, u32[]{:S(2)}, u32[]{:S(2)}) collective-permute-start(bf16[256,1,128]{0,2,1:T(8,128)(2,1)S(1)} %get-tuple-element.16), channel_id=1, source_target_pairs={{0,1},{1,2},{2,3},{3,4},{4,5},{5,6},{6,7},{7,8},{8,9},{9,10},{10,1... | collective-permute-start | bytes 196616 | tf_op jit(solution)/shard_map/ppermute | solution.py:160
  61.3 1.5 %collective-permute-start.2 = (bf16[256,1,128]{0,2,1:T(8,128)(2,1)S(1)}, bf16[256,1,128]{0,2,1:T(8,128)(2,1)S(1)}, u32[]{:S(2)}, u32[]{:S(2)}) collective-permute-start(bf16[256,1,128]{0,2,1:T(8,128)(2,1)S(1)} %get-tuple-element.17), channel_id=1, source_target_pairs={{1,0},{2,1},{3,2},{4,3},{5,4},{6,5},{7,6},{8,7},{9,8},{10,9},{11,1... | collective-permute-start | bytes 196616 | tf_op jit(solution)/shard_map/ppermute | solution.py:161
  62.9 2.1 %collective-permute-start.19 = (bf16[4,2,2,16,256]{4,3,0,2,1:T(8,128)(2,1)S(1)}, bf16[4,2,2,16,256]{4,3,0,2,1:T(8,128)(2,1)S(1)}, u32[]{:S(2)}, u32[]{:S(2)}) collective-permute-start(bf16[4,2,2,16,256]{4,3,0,2,1:T(8,128)(2,1)S(1)} %fusion.123), channel_id=1, source_target_pairs={{0,1},{1,0},{2,3},{3,2},{4,5},{5,4},{6,7},{7,6},{8,9},{9,8},{10,11... | collective-permute-start | bytes 393224 | tf_op jit(solution)/shard_map/ppermute | solution.py:110
  65.4 3.2 %collective-permute-start.16 = (bf16[4,2,2,16,256]{4,3,2,1,0:T(8,128)(2,1)S(1)}, bf16[4,2,2,16,256]{4,3,2,1,0:T(8,128)(2,1)S(1)}, u32[]{:S(2)}, u32[]{:S(2)}) collective-permute-start(bf16[4,2,2,16,256]{4,3,2,1,0:T(8,128)(2,1)S(1)} %fusion.122), channel_id=1, source_target_pairs={{0,1},{1,0},{2,3},{3,2},{4,5},{5,4},{6,7},{7,6},{8,9},{9,8},{10,11... | collective-permute-start | bytes 393224 | tf_op jit(solution)/shard_map/ppermute | solution.py:110
  75.4 1.8 %collective-permute-start.20 = (bf16[4,2,16,256]{3,2,0,1:T(8,128)(2,1)S(1)}, bf16[4,2,16,256]{3,2,0,1:T(8,128)(2,1)S(1)}, u32[]{:S(2)}, u32[]{:S(2)}) collective-permute-start(bf16[4,2,16,256]{3,2,0,1:T(8,128)(2,1)S(1)} %fusion.125), channel_id=1, source_target_pairs={{0,4},{1,5},{2,6},{3,7},{4,0},{5,1},{6,2},{7,3},{8,12},{9,13},{10,... | collective-permute-start | bytes 196616 | tf_op jit(solution)/shard_map/ppermute | solution.py:110
  77.2 3.2 %collective-permute-start.17 = (bf16[4,2,16,256]{3,2,1,0:T(8,128)(2,1)S(1)}, bf16[4,2,16,256]{3,2,1,0:T(8,128)(2,1)S(1)}, u32[]{:S(2)}, u32[]{:S(2)}) collective-permute-start(bf16[4,2,16,256]{3,2,1,0:T(8,128)(2,1)S(1)} %fusion.124), channel_id=1, source_target_pairs={{0,2},{1,3},{2,0},{3,1},{4,6},{5,7},{6,4},{7,5},{8,10},{9,11},{10,... | collective-permute-start | bytes 196616 | tf_op jit(solution)/shard_map/ppermute | solution.py:110
  80.5 2.6 %collective-permute-start.21 = (bf16[4,16,256]{2,1,0:T(8,128)(2,1)S(1)}, bf16[4,16,256]{2,1,0:T(8,128)(2,1)S(1)}, u32[]{:S(2)}, u32[]{:S(2)}) collective-permute-start(bf16[4,16,256]{2,1,0:T(8,128)(2,1)S(1)} %fusion.127), channel_id=1, source_target_pairs={{0,2},{1,3},{2,0},{3,1},{4,6},{5,7},{6,4},{7,5},{8,10},{9,11},{10,... | collective-permute-start | bytes 98312 | tf_op jit(solution)/shard_map/ppermute | solution.py:110
  83.1 1.6 %collective-permute-start.18 = (bf16[4,16,256]{2,1,0:T(8,128)(2,1)S(1)}, bf16[4,16,256]{2,1,0:T(8,128)(2,1)S(1)}, u32[]{:S(2)}, u32[]{:S(2)}) collective-permute-start(bf16[4,16,256]{2,1,0:T(8,128)(2,1)S(1)} %fusion.126), channel_id=1, source_target_pairs={{0,4},{1,5},{2,6},{3,7},{4,0},{5,1},{6,2},{7,3},{8,12},{9,13},{10,... | collective-permute-start | bytes 98312 | tf_op jit(solution)/shard_map/ppermute | solution.py:110
  85.0 1.3 collective-permute-start.3
  87.1 1.3 collective-permute-start.5
  88.5 6.6 %collective-permute-start.22 = (bf16[4,16,256]{2,1,0:T(8,128)(2,1)S(1)}, bf16[4,16,256]{2,1,0:T(8,128)(2,1)S(1)}, u32[]{:S(2)}, u32[]{:S(2)}) collective-permute-start(bf16[4,16,256]{2,1,0:T(8,128)(2,1)S(1)} %select_convert_fusion.1), channel_id=1, source_target_pairs={{0,8},{1,9},{2,10},{3,11},{4,12},{5,13},{6,14},{7,15},{8,0},{9,1},... | collective-permute-start | bytes 98312 | tf_op jit(solution)/shard_map/ppermute | solution.py:110
  95.1 2.8 %collective-permute-done.22 = bf16[4,16,256]{2,1,0:T(8,128)(2,1)S(1)} collective-permute-done((bf16[4,16,256]{2,1,0:T(8,128)(2,1)S(1)}, bf16[4,16,256]{2,1,0:T(8,128)(2,1)S(1)}, u32[]{:S(2)}, u32[]{:S(2)}) %collective-permute-start.22) | collective-permute-done | bytes 32800 | tf_op jit(solution)/shard_map/ppermute | solution.py:110
  107.1 1.6 %collective-permute-start.10 = (bf16[9,2,32,256]{3,2,0,1:T(8,128)(2,1)S(1)}, bf16[9,2,32,256]{3,2,0,1:T(8,128)(2,1)S(1)}, u32[]{:S(2)}, u32[]{:S(2)}) collective-permute-start(bf16[9,2,32,256]{3,2,0,1:T(8,128)(2,1)S(1)} %fusion.113), channel_id=1, source_target_pairs={{0,4},{1,5},{2,6},{3,7},{4,0},{5,1},{6,2},{7,3},{8,12},{9,13},{10,... | collective-permute-start | bytes 884744 | tf_op jit(solution)/shard_map/ppermute | solution.py:110
  108.8 6.5 %collective-permute-done.7 = bf16[9,2,32,256]{3,2,1,0:T(8,128)(2,1)S(1)} collective-permute-done((bf16[9,2,32,256]{3,2,1,0:T(8,128)(2,1)S(1)}, bf16[9,2,32,256]{3,2,1,0:T(8,128)(2,1)S(1)}, u32[]{:S(2)}, u32[]{:S(2)}) %collective-permute-start.7) | collective-permute-done | bytes 294944 | tf_op jit(solution)/shard_map/ppermute | solution.py:110
  119.0 1.7 %collective-permute-done.8 = bf16[9,32,256]{2,1,0:T(8,128)(2,1)S(1)} collective-permute-done((bf16[9,32,256]{2,1,0:T(8,128)(2,1)S(1)}, bf16[9,32,256]{2,1,0:T(8,128)(2,1)S(1)}, u32[]{:S(2)}, u32[]{:S(2)}) %collective-permute-start.8) | collective-permute-done | bytes 147488 | tf_op jit(solution)/shard_map/ppermute | solution.py:110
  122.6 2.0 %collective-permute-start.12 = (bf16[9,32,256]{2,1,0:T(8,128)(2,1)}, bf16[9,32,256]{2,1,0:T(8,128)(2,1)}, u32[]{:S(2)}, u32[]{:S(2)}) collective-permute-start(bf16[9,32,256]{2,1,0:T(8,128)(2,1)} %select_convert_fusion), channel_id=1, source_target_pairs={{0,8},{1,9},{2,10},{3,11},{4,12},{5,13},{6,14},{7,15},{8,0},{9,1},... | collective-permute-start | bytes 442376 | tf_op jit(solution)/shard_map/ppermute | solution.py:110
  124.5 1.4 %fusion.5 = bf16[128,8,2,128,2]{0,3,1,4,2:T(8,128)(2,1)S(1)} fusion(f32[2,2,128,8,128]{2,4,3,1,0:T(8,128)S(1)} %fusion.53, bf16[256,8,128]{0,2,1:T(8,128)(2,1)S(1)} %collective-permute-done.24, bf16[2,2,128,256]{3,2,1,0:T(8,128)(2,1)} %collective-permute-done.23), kind=kOutput, calls=%fused_computation.11 | convolution fusion | flops 269484032 | bytes 3932160 | tf_op jit(solution)/shard_map/drw,abcd->crawb/dot_general | solution.py:232
  127.1 1.7 %copy.246 = bf16[128,16,256]{2,1,0:T(8,128)(2,1)} copy(bf16[128,16,256]{0,2,1:T(8,128)(2,1)S(1)} %bitcast.360) | data formatting | bytes 2097152
  128.8 2.2 %copy.245 = bf16[256,8,128]{2,1,0:T(8,128)(2,1)} copy(bf16[256,8,128]{2,0,1:T(8,128)(2,1)} %fusion.19) | data formatting | bytes 1048576
  130.9 2.0 %add_multiply_fusion.1 = f32[9,32,256]{2,1,0:T(8,128)} fusion(bf16[9,32,256]{2,1,0:T(8,128)(2,1)} %collective-permute-done.12, bf16[9,32,256]{2,1,0:T(8,128)(2,1)S(1)} %collective-permute-done.8, f32[9,2,32,256]{3,2,1,0:T(8,128)} %copy-done.4, s32[]{:T(128)S(6)} %select_n.89, bf16[9,32,256]{2,1,0:T(8,128)(2,1)} %copy-done.7, ...), kind=kLoop, calls=%fused_computation.167 | loop fusion | flops 589824 | bytes 1327113 | tf_op jit(solution)/shard_map/mul | solution.py:220
  (151 shorter events, 35.8 us)
Async XLA Ops:
  0.6 16.0 %copy-start = (bf16[3,3,512,256]{3,2,1,0:T(8,128)(2,1)S(1)}, bf16[3,3,512,256]{3,2,1,0:T(8,128)(2,1)}, u32[]{:S(2)}) copy-start(bf16[3,3,512,256]{3,2,1,0:T(8,128)(2,1)} %param.6) | copy-start | bytes 7077892
  0.6 11.9 %copy-start.6 = (bf16[2,2,256,256]{3,2,1,0:T(8,128)(2,1)S(1)}, bf16[2,2,256,256]{3,2,1,0:T(8,128)(2,1)}, u32[]{:S(2)}) copy-start(bf16[2,2,256,256]{3,2,1,0:T(8,128)(2,1)} %param.5) | copy-start | bytes 1572868
  2.6 13.4 %collective-permute-start.14 = (bf16[256,1,128]{2,0,1:T(8,128)(2,1)}, bf16[256,1,128]{2,0,1:T(8,128)(2,1)S(1)}, u32[]{:S(2)}, u32[]{:S(2)}) collective-permute-start(bf16[256,1,128]{2,0,1:T(8,128)(2,1)} %get-tuple-element.13), channel_id=1, source_target_pairs={{1,0},{2,1},{3,2},{4,3},{5,4},{6,5},{7,6},{8,7},{9,8},{10,9},{11,1... | collective-permute-start | bytes 196616 | tf_op jit(solution)/shard_map/ppermute | solution.py:161
  3.9 12.1 %collective-permute-start.13 = (bf16[256,1,128]{2,0,1:T(8,128)(2,1)}, bf16[256,1,128]{2,0,1:T(8,128)(2,1)S(1)}, u32[]{:S(2)}, u32[]{:S(2)}) collective-permute-start(bf16[256,1,128]{2,0,1:T(8,128)(2,1)} %get-tuple-element.12), channel_id=1, source_target_pairs={{0,1},{1,2},{2,3},{3,4},{4,5},{5,6},{6,7},{7,8},{8,9},{9,10},{10,1... | collective-permute-start | bytes 196616 | tf_op jit(solution)/shard_map/ppermute | solution.py:160
  9.6 26.7 %collective-permute-start = (bf16[128,16,256]{0,2,1:T(8,128)(2,1)}, bf16[128,16,256]{0,2,1:T(8,128)(2,1)}, u32[]{:S(2)}, u32[]{:S(2)}) collective-permute-start(bf16[128,16,256]{0,2,1:T(8,128)(2,1)} %copy.126), channel_id=1, source_target_pairs={{0,16},{16,0},{1,17},{17,1},{2,18},{18,2},{3,19},{19,3},{4,20},{20... | collective-permute-start | bytes 3145736 | tf_op jit(solution)/shard_map/ppermute | solution.py:110
  13.3 111.2 %collective-permute-start.23 = (bf16[2,2,128,256]{3,2,1,0:T(8,128)(2,1)}, bf16[2,2,128,256]{3,2,1,0:T(8,128)(2,1)}, u32[]{:S(2)}, u32[]{:S(2)}) collective-permute-start(bf16[2,2,128,256]{3,2,1,0:T(8,128)(2,1)} %constant_dynamic-slice_fusion.4), channel_id=1, source_target_pairs={{0,16},{16,0},{1,17},{17,1},{2,18},{18,2},{3,19},{19,3},{4,20},{20... | collective-permute-start | bytes 786440 | tf_op jit(solution)/shard_map/ppermute | solution.py:110
  20.8 32.2 %collective-permute-start.15 = (bf16[256,8,128]{0,2,1:T(8,128)(2,1)S(1)}, bf16[256,8,128]{0,2,1:T(8,128)(2,1)S(1)}, u32[]{:S(2)}, u32[]{:S(2)}) collective-permute-start(bf16[256,8,128]{0,2,1:T(8,128)(2,1)S(1)} %fusion.18), channel_id=1, source_target_pairs={{0,16},{16,0},{1,17},{17,1},{2,18},{18,2},{3,19},{19,3},{4,20},{20... | collective-permute-start | bytes 1572872 | tf_op jit(solution)/shard_map/ppermute | solution.py:110
  25.6 10.7 %copy-start.3 = (f32[256,8,128]{0,2,1:T(8,128)S(1)}, f32[256,8,128]{0,2,1:T(8,128)}, u32[]{:S(2)}) copy-start(f32[256,8,128]{0,2,1:T(8,128)} %convolution_bitcast_fusion.1) | copy-start | bytes 3145732
  53.8 4.8 %copy-start.2 = (bf16[128,16,256]{0,2,1:T(8,128)(2,1)S(1)}, bf16[128,16,256]{0,2,1:T(8,128)(2,1)}, u32[]{:S(2)}) copy-start(bf16[128,16,256]{0,2,1:T(8,128)(2,1)} %copy.126) | copy-start | bytes 3145732
  54.3 70.3 %collective-permute-start.24 = (bf16[256,8,128]{0,2,1:T(8,128)(2,1)S(1)}, bf16[256,8,128]{0,2,1:T(8,128)(2,1)S(1)}, u32[]{:S(2)}, u32[]{:S(2)}) collective-permute-start(bf16[256,8,128]{0,2,1:T(8,128)(2,1)S(1)} %fusion.17), channel_id=1, source_target_pairs={{0,16},{16,0},{1,17},{17,1},{2,18},{18,2},{3,19},{19,3},{4,20},{20... | collective-permute-start | bytes 1572872 | tf_op jit(solution)/shard_map/ppermute | solution.py:110
  59.1 39.5 %collective-permute-start.4 = (bf16[256,8,128]{0,2,1:T(8,128)(2,1)S(1)}, bf16[256,8,128]{0,2,1:T(8,128)(2,1)S(1)}, u32[]{:S(2)}, u32[]{:S(2)}) collective-permute-start(bf16[256,8,128]{0,2,1:T(8,128)(2,1)S(1)} %get-tuple-element.18), channel_id=1, source_target_pairs={{0,16},{16,0},{1,17},{17,1},{2,18},{18,2},{3,19},{19,3},{4,20},{20... | collective-permute-start | bytes 1572872 | tf_op jit(solution)/shard_map/ppermute | solution.py:110
  59.6 3.3 %collective-permute-start.1 = (bf16[256,1,128]{0,2,1:T(8,128)(2,1)S(1)}, bf16[256,1,128]{0,2,1:T(8,128)(2,1)S(1)}, u32[]{:S(2)}, u32[]{:S(2)}) collective-permute-start(bf16[256,1,128]{0,2,1:T(8,128)(2,1)S(1)} %get-tuple-element.16), channel_id=1, source_target_pairs={{0,1},{1,2},{2,3},{3,4},{4,5},{5,6},{6,7},{7,8},{8,9},{9,10},{10,1... | collective-permute-start | bytes 196616 | tf_op jit(solution)/shard_map/ppermute | solution.py:160
  61.3 4.0 %collective-permute-start.2 = (bf16[256,1,128]{0,2,1:T(8,128)(2,1)S(1)}, bf16[256,1,128]{0,2,1:T(8,128)(2,1)S(1)}, u32[]{:S(2)}, u32[]{:S(2)}) collective-permute-start(bf16[256,1,128]{0,2,1:T(8,128)(2,1)S(1)} %get-tuple-element.17), channel_id=1, source_target_pairs={{1,0},{2,1},{3,2},{4,3},{5,4},{6,5},{7,6},{8,7},{9,8},{10,9},{11,1... | collective-permute-start | bytes 196616 | tf_op jit(solution)/shard_map/ppermute | solution.py:161
  62.9 12.4 %collective-permute-start.19 = (bf16[4,2,2,16,256]{4,3,0,2,1:T(8,128)(2,1)S(1)}, bf16[4,2,2,16,256]{4,3,0,2,1:T(8,128)(2,1)S(1)}, u32[]{:S(2)}, u32[]{:S(2)}) collective-permute-start(bf16[4,2,2,16,256]{4,3,0,2,1:T(8,128)(2,1)S(1)} %fusion.123), channel_id=1, source_target_pairs={{0,1},{1,0},{2,3},{3,2},{4,5},{5,4},{6,7},{7,6},{8,9},{9,8},{10,11... | collective-permute-start | bytes 393224 | tf_op jit(solution)/shard_map/ppermute | solution.py:110
  65.4 11.8 %collective-permute-start.16 = (bf16[4,2,2,16,256]{4,3,2,1,0:T(8,128)(2,1)S(1)}, bf16[4,2,2,16,256]{4,3,2,1,0:T(8,128)(2,1)S(1)}, u32[]{:S(2)}, u32[]{:S(2)}) collective-permute-start(bf16[4,2,2,16,256]{4,3,2,1,0:T(8,128)(2,1)S(1)} %fusion.122), channel_id=1, source_target_pairs={{0,1},{1,0},{2,3},{3,2},{4,5},{5,4},{6,7},{7,6},{8,9},{9,8},{10,11... | collective-permute-start | bytes 393224 | tf_op jit(solution)/shard_map/ppermute | solution.py:110
  75.4 5.1 %collective-permute-start.20 = (bf16[4,2,16,256]{3,2,0,1:T(8,128)(2,1)S(1)}, bf16[4,2,16,256]{3,2,0,1:T(8,128)(2,1)S(1)}, u32[]{:S(2)}, u32[]{:S(2)}) collective-permute-start(bf16[4,2,16,256]{3,2,0,1:T(8,128)(2,1)S(1)} %fusion.125), channel_id=1, source_target_pairs={{0,4},{1,5},{2,6},{3,7},{4,0},{5,1},{6,2},{7,3},{8,12},{9,13},{10,... | collective-permute-start | bytes 196616 | tf_op jit(solution)/shard_map/ppermute | solution.py:110
  77.2 5.9 %collective-permute-start.17 = (bf16[4,2,16,256]{3,2,1,0:T(8,128)(2,1)S(1)}, bf16[4,2,16,256]{3,2,1,0:T(8,128)(2,1)S(1)}, u32[]{:S(2)}, u32[]{:S(2)}) collective-permute-start(bf16[4,2,16,256]{3,2,1,0:T(8,128)(2,1)S(1)} %fusion.124), channel_id=1, source_target_pairs={{0,2},{1,3},{2,0},{3,1},{4,6},{5,7},{6,4},{7,5},{8,10},{9,11},{10,... | collective-permute-start | bytes 196616 | tf_op jit(solution)/shard_map/ppermute | solution.py:110
  80.5 4.5 %collective-permute-start.21 = (bf16[4,16,256]{2,1,0:T(8,128)(2,1)S(1)}, bf16[4,16,256]{2,1,0:T(8,128)(2,1)S(1)}, u32[]{:S(2)}, u32[]{:S(2)}) collective-permute-start(bf16[4,16,256]{2,1,0:T(8,128)(2,1)S(1)} %fusion.127), channel_id=1, source_target_pairs={{0,2},{1,3},{2,0},{3,1},{4,6},{5,7},{6,4},{7,5},{8,10},{9,11},{10,... | collective-permute-start | bytes 98312 | tf_op jit(solution)/shard_map/ppermute | solution.py:110
  83.1 4.0 %collective-permute-start.18 = (bf16[4,16,256]{2,1,0:T(8,128)(2,1)S(1)}, bf16[4,16,256]{2,1,0:T(8,128)(2,1)S(1)}, u32[]{:S(2)}, u32[]{:S(2)}) collective-permute-start(bf16[4,16,256]{2,1,0:T(8,128)(2,1)S(1)} %fusion.126), channel_id=1, source_target_pairs={{0,4},{1,5},{2,6},{3,7},{4,0},{5,1},{6,2},{7,3},{8,12},{9,13},{10,... | collective-permute-start | bytes 98312 | tf_op jit(solution)/shard_map/ppermute | solution.py:110
  85.0 3.5 %collective-permute-start.3 = (bf16[256,1,128]{0,2,1:T(8,128)(2,1)S(1)}, bf16[256,1,128]{0,2,1:T(8,128)(2,1)S(1)}, u32[]{:S(2)}, u32[]{:S(2)}) collective-permute-start(bf16[256,1,128]{0,2,1:T(8,128)(2,1)S(1)} %get-tuple-element.16), channel_id=1, source_target_pairs={{0,17},{1,18},{2,19},{3,20},{4,21},{5,22},{6,23},{7,24},{8,25},{9,... | collective-permute-start | bytes 196616 | tf_op jit(solution)/shard_map/ppermute | solution.py:160
  87.1 11.5 %collective-permute-start.5 = (bf16[256,1,128]{0,2,1:T(8,128)(2,1)S(1)}, bf16[256,1,128]{0,2,1:T(8,128)(2,1)S(1)}, u32[]{:S(2)}, u32[]{:S(2)}) collective-permute-start(bf16[256,1,128]{0,2,1:T(8,128)(2,1)S(1)} %get-tuple-element.17), channel_id=1, source_target_pairs={{1,16},{2,17},{3,18},{4,19},{5,20},{6,21},{7,22},{8,23},{9,24},{10... | collective-permute-start | bytes 196616 | tf_op jit(solution)/shard_map/ppermute | solution.py:161
  88.5 9.4 %collective-permute-start.22 = (bf16[4,16,256]{2,1,0:T(8,128)(2,1)S(1)}, bf16[4,16,256]{2,1,0:T(8,128)(2,1)S(1)}, u32[]{:S(2)}, u32[]{:S(2)}) collective-permute-start(bf16[4,16,256]{2,1,0:T(8,128)(2,1)S(1)} %select_convert_fusion.1), channel_id=1, source_target_pairs={{0,8},{1,9},{2,10},{3,11},{4,12},{5,13},{6,14},{7,15},{8,0},{9,1},... | collective-permute-start | bytes 98312 | tf_op jit(solution)/shard_map/ppermute | solution.py:110
  97.9 8.1 %collective-permute-start.6 = (bf16[9,2,2,32,256]{4,3,2,1,0:T(8,128)(2,1)S(1)}, bf16[9,2,2,32,256]{4,3,2,1,0:T(8,128)(2,1)S(1)}, u32[]{:S(2)}, u32[]{:S(2)}) collective-permute-start(bf16[9,2,2,32,256]{4,3,2,1,0:T(8,128)(2,1)S(1)} %fusion.32), channel_id=1, source_target_pairs={{0,1},{1,0},{2,3},{3,2},{4,5},{5,4},{6,7},{7,6},{8,9},{9,8},{10,11... | collective-permute-start | bytes 1769480 | tf_op jit(solution)/shard_map/ppermute | solution.py:110
  103.2 3.6 %collective-permute-start.9 = (bf16[9,2,2,32,256]{4,3,0,2,1:T(8,128)(2,1)S(1)}, bf16[9,2,2,32,256]{4,3,0,2,1:T(8,128)(2,1)S(1)}, u32[]{:S(2)}, u32[]{:S(2)}) collective-permute-start(bf16[9,2,2,32,256]{4,3,0,2,1:T(8,128)(2,1)S(1)} %fusion.33), channel_id=1, source_target_pairs={{0,1},{1,0},{2,3},{3,2},{4,5},{5,4},{6,7},{7,6},{8,9},{9,8},{10,11... | collective-permute-start | bytes 1769480 | tf_op jit(solution)/shard_map/ppermute | solution.py:110
  106.3 9.0 %collective-permute-start.7 = (bf16[9,2,32,256]{3,2,1,0:T(8,128)(2,1)S(1)}, bf16[9,2,32,256]{3,2,1,0:T(8,128)(2,1)S(1)}, u32[]{:S(2)}, u32[]{:S(2)}) collective-permute-start(bf16[9,2,32,256]{3,2,1,0:T(8,128)(2,1)S(1)} %fusion.112), channel_id=1, source_target_pairs={{0,2},{1,3},{2,0},{3,1},{4,6},{5,7},{6,4},{7,5},{8,10},{9,11},{10,... | collective-permute-start | bytes 884744 | tf_op jit(solution)/shard_map/ppermute | solution.py:110
  107.1 9.4 %collective-permute-start.10 = (bf16[9,2,32,256]{3,2,0,1:T(8,128)(2,1)S(1)}, bf16[9,2,32,256]{3,2,0,1:T(8,128)(2,1)S(1)}, u32[]{:S(2)}, u32[]{:S(2)}) collective-permute-start(bf16[9,2,32,256]{3,2,0,1:T(8,128)(2,1)S(1)} %fusion.113), channel_id=1, source_target_pairs={{0,4},{1,5},{2,6},{3,7},{4,0},{5,1},{6,2},{7,3},{8,12},{9,13},{10,... | collective-permute-start | bytes 884744 | tf_op jit(solution)/shard_map/ppermute | solution.py:110
  115.4 9.1 %copy-start.4 = (f32[9,2,32,256]{3,2,1,0:T(8,128)}, f32[9,2,32,256]{3,2,1,0:T(8,128)S(1)}, u32[]{:S(2)}) copy-start(f32[9,2,32,256]{3,2,1,0:T(8,128)S(1)} %bitcast_add_fusion.2) | copy-start | bytes 1769476
  115.4 5.2 %collective-permute-start.8 = (bf16[9,32,256]{2,1,0:T(8,128)(2,1)S(1)}, bf16[9,32,256]{2,1,0:T(8,128)(2,1)S(1)}, u32[]{:S(2)}, u32[]{:S(2)}) collective-permute-start(bf16[9,32,256]{2,1,0:T(8,128)(2,1)S(1)} %fusion.120), channel_id=1, source_target_pairs={{0,4},{1,5},{2,6},{3,7},{4,0},{5,1},{6,2},{7,3},{8,12},{9,13},{10,... | collective-permute-start | bytes 442376 | tf_op jit(solution)/shard_map/ppermute | solution.py:110
  116.6 10.5 %copy-start.5 = (f32[9,2,32,256]{3,2,0,1:T(8,128)}, f32[9,2,32,256]{3,2,0,1:T(8,128)S(1)}, u32[]{:S(2)}) copy-start(f32[9,2,32,256]{3,2,0,1:T(8,128)S(1)} %bitcast_add_fusion.1) | copy-start | bytes 1769476
  116.6 5.2 %collective-permute-start.11 = (bf16[9,32,256]{2,1,0:T(8,128)(2,1)S(1)}, bf16[9,32,256]{2,1,0:T(8,128)(2,1)S(1)}, u32[]{:S(2)}, u32[]{:S(2)}) collective-permute-start(bf16[9,32,256]{2,1,0:T(8,128)(2,1)S(1)} %fusion.121), channel_id=1, source_target_pairs={{0,2},{1,3},{2,0},{3,1},{4,6},{5,7},{6,4},{7,5},{8,10},{9,11},{10,... | collective-permute-start | bytes 442376 | tf_op jit(solution)/shard_map/ppermute | solution.py:110
  121.8 2.7 %copy-start.7 = (bf16[9,32,256]{2,1,0:T(8,128)(2,1)}, bf16[9,32,256]{2,1,0:T(8,128)(2,1)S(1)}, u32[]{:S(2)}) copy-start(bf16[9,32,256]{2,1,0:T(8,128)(2,1)S(1)} %collective-permute-done.11) | copy-start | bytes 442372
  122.6 8.4 %collective-permute-start.12 = (bf16[9,32,256]{2,1,0:T(8,128)(2,1)}, bf16[9,32,256]{2,1,0:T(8,128)(2,1)}, u32[]{:S(2)}, u32[]{:S(2)}) collective-permute-start(bf16[9,32,256]{2,1,0:T(8,128)(2,1)} %select_convert_fusion), channel_id=1, source_target_pairs={{0,8},{1,9},{2,10},{3,11},{4,12},{5,13},{6,14},{7,15},{8,0},{9,1},... | collective-permute-start | bytes 442376 | tf_op jit(solution)/shard_map/ppermute | solution.py:110
  (1 other events, 1.0 us)

commit v2 on v1

--- a/solution.py
+++ b/solution.py
@@ -130,7 +130,7 @@
     return keep.astype(jnp.float32) + got.astype(jnp.float32)
 
 
-def reduce_halves(own, other, top):
+def reduce_halves(own, other, top, swapped=None):
     taps, half, depth = own.shape
     share = half >> top
     own_bits = list(range(top))
@@ -143,10 +143,13 @@
             block = halve(block, 1 + left.index(bit), bit)
             left.remove(bit)
         sums.append(block)
+    if swapped is not None:
+        sums, swapped = lax.optimization_barrier((sums, swapped))
     here = (lax.axis_index("tile") >> top) == lax.axis_index("chan")
     keep = jnp.where(here, sums[0], sums[1])
     send = jnp.where(here, sums[1], sums[0])
-    return keep + flip(send.astype(jnp.bfloat16), "tile", 1 << top).astype(jnp.float32)
+    total = keep + flip(send.astype(jnp.bfloat16), "tile", 1 << top).astype(jnp.float32)
+    return total if swapped is None else (total, swapped)
 
 
 def edge_rows(block, cross):
@@ -179,27 +182,29 @@
     def part(weights, which, dim, size):
         return lax.dynamic_slice_in_dim(weights, which * size, size, dim)
 
-    image_far = flip(image, "chan", 1)
+    deep, cotangent = lax.optimization_barrier((image.transpose(1, 2, 0), cotangent))
+    deep_far = flip(deep, "chan", 1)
     cot_edges = edge_rows(cotangent, False)
     down_own, down_far = part(w_down, k, 2, own_in), part(w_down, 1 - k, 2, own_in)
     mix_own, mix_far = part(w_mix, k, 2, own_out), part(w_mix, 1 - k, 2, own_out)
-    down_back = flip(down_far, "chan", 1)
 
     cot_pad = rimmed(cotangent, cot_edges)
-    away = tap_sum(cot_pad, mix_far, n_rows, n_cols, True)
-    got = flip(away.astype(bf16), "chan", 1)
+    away = tap_sum(cot_pad, mix_far, n_rows, n_cols, True).astype(bf16)
     grad_hidden = tap_sum(cot_pad, mix_own, n_rows, n_cols, True)
 
     def taps_of(block):
-        return block.reshape(own_in, n_rows, 2, n_cols, 2)
-
-    near, far = taps_of(image), taps_of(image_far)
-    preact = jnp.einsum("crawb,abcd->drw", near, down_own, preferred_element_type=f32)
-    preact = preact + jnp.einsum("crawb,abcd->drw", far, down_far, preferred_element_type=f32)
+        return block.reshape(n_rows, 2, n_cols, 2, own_in)
+
+    near, far = taps_of(deep), taps_of(deep_far)
+    preact = jnp.einsum("rawbc,abcd->drw", near, down_own, preferred_element_type=f32)
+    preact = preact + jnp.einsum("rawbc,abcd->drw", far, down_far, preferred_element_type=f32)
     cdf = normal_cdf(preact)
     hidden = (preact * cdf).astype(bf16)
     hidden_far = flip(hidden, "chan", 1)
     own_edges, far_edges = edge_rows(hidden, False), edge_rows(hidden, True)
+    hidden_far, away, down_far = lax.optimization_barrier((hidden_far, away, down_far))
+    got = flip(away, "chan", 1)
+    down_back = flip(down_far, "chan", 1)
 
     slope = cdf + preact * normal_pdf(preact)
     grad_pre = ((grad_hidden + got.astype(f32)) * slope).astype(bf16)
@@ -223,11 +228,13 @@
     mixed = (mixed + tap_sum(far_pad, mix_far, n_rows, n_cols, False)).astype(bf16)
 
     def down_terms(patches):
-        term = jnp.einsum("crawb,drw->abcd", patches, grad_pre, preferred_element_type=f32)
+        term = jnp.einsum("rawbc,drw->abcd", patches, grad_pre, preferred_element_type=f32)
         return term.reshape(4, own_in, own_out)
 
-    grad_down = reduce_halves(down_terms(near), down_terms(far), top) * scale
-    grad_down = grad_down.transpose(1, 0, 2).reshape(-1, 2, 2, own_out)
+    grad_down, grad_pre_far = reduce_halves(
+        down_terms(near), down_terms(far), top, grad_pre_far
+    )
+    grad_down = (grad_down * scale).transpose(1, 0, 2).reshape(-1, 2, 2, own_out)
     term = jnp.einsum("drw,abcd->crawb", grad_pre, down_own, preferred_element_type=f32)
     term = term + jnp.einsum(
         "drw,abcd->crawb", grad_pre_far, down_back, preferred_element_type=f32

time: 133 us -> 133 us (level)
  starting transfers between devices: 46 us -> 38.5 us
  local copies, waits for them, and re-layouts: 11.9 us -> 18.6 us
  waiting for transfers between devices: 38.3 us -> 32.5 us
  matrix products: 30.7 us -> 33.5 us
  other arithmetic: 4.49 us -> 7.12 us
    ppermute x19, starting transfers between devices: 35.8 us -> 27.1 us  [flip(): return lax.ppermute(block, axis, [(i, i ^ mask) for i in range(count)])]
    ppermute x19, waiting for transfers between devices: 37.8 us -> 32.3 us  [flip(): return lax.ppermute(block, axis, [(i, i ^ mask) for i in range(count)])]
    dot_general x0 -> x2, local copies, waits for them, and re-layouts: none -> 5.36 us  [down_terms(): jnp.einsum('rawbc,drw->abcd', patches, grad_pre, preferred_element_type=f32)]
    dot_general x36, matrix products: 15.7 us -> 19 us  [tap_sum(): jnp.einsum(form, window, weights[i, j], preferred_element_type=jnp.float32)]
    dot_general x18, matrix products: 6.47 us -> 8.19 us  [mix_terms(): jnp.einsum('crw,drw->cd', window, cotangent, preferred_element_type=f32)]
    ppermute x3, starting transfers between devices: 6.09 us -> 7.53 us  [edge_rows(): low = lax.ppermute(block[:, -1:], ('chan', 'tile'), down)]
    dot_general x4, matrix products: 6.72 us -> 5.35 us  [the longest x1 2.68 us: pair_device(): jnp.einsum('rawbc,abcd->drw', far, down_far, preferred_element_type=f32)]
    unnamed x38 -> x66, local copies, waits for them, and re-layouts: 8.27 us -> 9.34 us
  transfers between devices with their start and end apart: 25 -> 25, of which waited for: 9 -> 10; matrix products, arithmetic and copies ran while one was open for 32% -> 38% of each run, Pallas kernels for 0% -> 0%
where the time goes in v2:
time: 133 us; the launch traced here: 132 us
  starting transfers between devices  38.5 us (29%)
  matrix products  33.5 us (25%)
  waiting for transfers between devices  32.5 us (24%)
  local copies, waits for them, and re-layouts  18.6 us (14%)
  other arithmetic  7.12 us (5%)
  between operations  1.73 us (1%)
    ppermute x19, waiting for transfers between devices, flip(): return lax.ppermute(block, axis, [(i, i ^ mask) for i in range(count)])  32.3 us
    ppermute x19, starting transfers between devices, flip(): return lax.ppermute(block, axis, [(i, i ^ mask) for i in range(count)])  27.1 us
    dot_general x36, matrix products, tap_sum(): jnp.einsum(form, window, weights[i, j], preferred_element_type=jnp.float32)  19 us
    unnamed x66, local copies, waits for them, and re-layouts  9.34 us
    dot_general x18, matrix products, mix_terms(): jnp.einsum('crw,drw->cd', window, cotangent, preferred_element_type=f32)  8.19 us
    ppermute x3, starting transfers between devices, edge_rows(): low = lax.ppermute(block[:, -1:], ('chan', 'tile'), down)  7.53 us
    dot_general x2, local copies, waits for them, and re-layouts, down_terms(): jnp.einsum('rawbc,drw->abcd', patches, grad_pre, preferred_element_type=f32)  5.36 us
    ppermute x3, starting transfers between devices, edge_rows(): high = lax.ppermute(block[:, :1], ('chan', 'tile'), up)  3.86 us
  transfers between devices with their start and end apart: 25, of which 10 were waited for; matrix products, arithmetic and copies ran while one was open for 38% of the time, Pallas kernels for 0%

profile of v2, /device:TPU:0, one launch (start us, length us, event | category | flops | bytes accessed | tf_op | source)
XLA Modules:
  0.0 131.9 jit_solution(17064195574697189524)
XLA Ops:
  0.7 2.8 %copy.124 = bf16[128,16,256]{0,2,1:T(8,128)(2,1)} copy(bf16[128,16,256]{2,1,0:T(8,128)(2,1)} %param.4) | data formatting | bytes 2097152 | tf_op args[0]
  5.6 3.0 %collective-permute-start.5 = (bf16[256,1,128]{2,0,1:T(8,128)(2,1)}, bf16[256,1,128]{2,0,1:T(8,128)(2,1)S(1)}, u32[]{:S(2)}, u32[]{:S(2)}) collective-permute-start(bf16[256,1,128]{2,0,1:T(8,128)(2,1)} %get-tuple-element.30), channel_id=1, source_target_pairs={{0,1},{1,2},{2,3},{3,4},{4,5},{5,6},{6,7},{7,8},{8,9},{9,10},{10,1... | collective-permute-start | bytes 196616 | tf_op jit(solution)/shard_map/ppermute | solution.py:163
  8.6 3.0 %collective-permute-start = (bf16[16,256,128]{2,1,0:T(8,128)(2,1)}, bf16[16,256,128]{2,1,0:T(8,128)(2,1)}, u32[]{:S(2)}, u32[]{:S(2)}) collective-permute-start(bf16[16,256,128]{2,1,0:T(8,128)(2,1)} %bitcast.333), channel_id=1, source_target_pairs={{0,16},{16,0},{1,17},{17,1},{2,18},{18,2},{3,19},{19,3},{4,20},{20... | collective-permute-start | bytes 3145736 | tf_op jit(solution)/shard_map/ppermute | solution.py:110
  11.7 2.7 %copy.214 = bf16[2,2,128,8,128]{4,3,2,1,0:T(8,128)(2,1)} copy(bf16[2,2,128,8,128]{2,1,4,0,3:T(2,128)(2,1)} %bitcast.334) | data formatting | bytes 2097152 | tf_op jit(solution)/shard_map/rawbc,drw->abcd/dot_general | solution.py:231
  14.4 1.8 %convolution_bitcast_fusion.1 = f32[256,8,128]{0,2,1:T(8,128)S(1)} fusion(bf16[8,2,128,2,128]{4,3,2,1,0:T(2,128)(2,1)} %bitcast.335, bf16[2,2,256,256]{3,2,1,0:T(8,128)(2,1)} %param.5, s32[]{:T(128)S(6)} %select_n.81), kind=kOutput, calls=%fused_computation.48 | convolution fusion | flops 268435456 | bytes 2359300 | tf_op jit(solution)/shard_map/rawbc,abcd->drw/dot_general | solution.py:199
  19.7 1.6 %convolution_add_fusion.1 = f32[256,8,128]{0,2,1:T(8,128)} fusion(f32[256,8,128]{0,2,1:T(8,128)S(1)} %convolution_add_fusion.2, bf16[256,10,130]{2,0,1:T(8,128)(2,1)S(1)} %fusion.15, bf16[3,3,512,256]{3,2,1,0:T(8,128)(2,1)S(1)} %copy-done, s32[]{:T(128)S(6)} %add.289, s32[]{:T(128)S(6)} %select_n.80), kind=kOutput, calls=%fused_computation.16 | convolution fusion | flops 134479872 | bytes 2752520 | tf_op jit(solution)/shard_map/drw,cd->crw/dot_general | solution.py:120
  24.0 1.4 %fusion.75 = f32[256,8,128]{0,2,1:T(8,128)} fusion(bf16[256,10,130]{2,0,1:T(8,128)(2,1)S(1)} %fusion.15, bf16[3,3,512,256]{3,2,1,0:T(8,128)(2,1)S(1)} %copy-done, s32[]{:T(128)S(6)} %add.289, s32[]{:T(128)S(6)} %select_n.80), kind=kOutput, calls=%fused_computation.128 | convolution fusion | flops 134217728 | bytes 1703944 | tf_op jit(solution)/shard_map/drw,cd->crw/dot_general | solution.py:120
  27.6 7.8 %collective-permute-done = bf16[16,256,128]{2,1,0:T(8,128)(2,1)} collective-permute-done((bf16[16,256,128]{2,1,0:T(8,128)(2,1)}, bf16[16,256,128]{2,1,0:T(8,128)(2,1)}, u32[]{:S(2)}, u32[]{:S(2)}) %collective-permute-start) | collective-permute-done | bytes 1048608 | tf_op jit(solution)/shard_map/ppermute | solution.py:110
  35.4 2.7 %multiply_convert_fusion = (bf16[256,8,128]{0,2,1:T(8,128)(2,1)S(1)}, f32[256,8,128]{0,2,1:T(8,128)}) fusion(f32[256,8,128]{0,2,1:T(8,128)S(1)} %convolution_bitcast_fusion.1, bf16[8,2,128,2,128]{4,3,2,1,0:T(2,128)(2,1)} %bitcast.10, bf16[2,2,128,256]{3,2,1,0:T(8,128)(2,1)S(1)} %constant_dynamic-slice_fusion.4), kind=kOutput, calls=%fused_computation.70 | convolution fusion | flops 270008320 | bytes 3932160 | tf_op jit(solution)/shard_map/rawbc,abcd->drw/dot_general | solution.py:200
  38.1 2.5 %collective-permute-start.4 = (bf16[256,8,128]{0,2,1:T(8,128)(2,1)S(1)}, bf16[256,8,128]{0,2,1:T(8,128)(2,1)}, u32[]{:S(2)}, u32[]{:S(2)}) collective-permute-start(bf16[256,8,128]{0,2,1:T(8,128)(2,1)S(1)} %get-tuple-element.34), channel_id=1, source_target_pairs={{0,16},{16,0},{1,17},{17,1},{2,18},{18,2},{3,19},{19,3},{4,20},{20... | collective-permute-start | bytes 1572872 | tf_op jit(solution)/shard_map/ppermute | solution.py:110
  41.2 2.2 %collective-permute-start.3 = (bf16[256,1,128]{0,2,1:T(8,128)(2,1)}, bf16[256,1,128]{0,2,1:T(8,128)(2,1)}, u32[]{:S(2)}, u32[]{:S(2)}) collective-permute-start(bf16[256,1,128]{0,2,1:T(8,128)(2,1)} %get-tuple-element.32), channel_id=1, source_target_pairs={{0,17},{1,18},{2,19},{3,20},{4,21},{5,22},{6,23},{7,24},{8,25},{9,... | collective-permute-start | bytes 196616 | tf_op jit(solution)/shard_map/ppermute | solution.py:163
  43.4 2.3 %collective-permute-start.1 = (bf16[256,1,128]{0,2,1:T(8,128)(2,1)}, bf16[256,1,128]{0,2,1:T(8,128)(2,1)S(1)}, u32[]{:S(2)}, u32[]{:S(2)}) collective-permute-start(bf16[256,1,128]{0,2,1:T(8,128)(2,1)} %get-tuple-element.32), channel_id=1, source_target_pairs={{0,1},{1,2},{2,3},{3,4},{4,5},{5,6},{6,7},{7,8},{8,9},{9,10},{10,1... | collective-permute-start | bytes 196616 | tf_op jit(solution)/shard_map/ppermute | solution.py:163
  49.4 2.7 %copy.236 = bf16[2,2,128,8,128]{4,3,2,1,0:T(8,128)(2,1)} copy(bf16[2,2,128,8,128]{2,1,4,0,3:T(2,128)(2,1)} %bitcast.135) | data formatting | bytes 2097152 | tf_op jit(solution)/shard_map/rawbc,drw->abcd/dot_general | solution.py:231
  56.1 3.0 %collective-permute-start.8 = (bf16[9,2,2,32,256]{4,3,2,1,0:T(8,128)(2,1)S(1)}, bf16[9,2,2,32,256]{4,3,2,1,0:T(8,128)(2,1)S(1)}, u32[]{:S(2)}, u32[]{:S(2)}) collective-permute-start(bf16[9,2,2,32,256]{4,3,2,1,0:T(8,128)(2,1)S(1)} %fusion.30), channel_id=1, source_target_pairs={{0,1},{1,0},{2,3},{3,2},{4,5},{5,4},{6,7},{7,6},{8,9},{9,8},{10,11... | collective-permute-start | bytes 1769480 | tf_op jit(solution)/shard_map/ppermute | solution.py:110
  65.6 1.4 %fusion.178 = f32[256,256,1]{1,0,2:T(8,128)S(1)} fusion(bf16[256,8,128]{0,2,1:T(8,128)(2,1)} %collective-permute-done.4, bf16[256,8,128]{2,1,0:T(8,128)(2,1)S(1)} %copy-done.1), kind=kOutput, calls=%fused_computation.296 | convolution fusion | flops 134217728 | bytes 1310720 | tf_op jit(solution)/shard_map/crw,drw->cd/dot_general | solution.py:219
  75.5 1.4 %fusion.11 = f32[256,8,128]{2,0,1:T(8,128)S(1)} fusion(f32[256,8,128]{2,0,1:T(8,128)S(1)} %fusion.64, f32[256,8,128]{2,0,1:T(8,128)S(1)} %convolution_add_fusion.10, bf16[256,8,128]{0,2,1:T(8,128)(2,1)} %collective-permute-done.4, bf16[3,3,512,256]{3,2,1,0:T(8,128)(2,1)S(1)} %copy-done, s32[]{:T(128)S(6)} %add.288, s32[]{:T(128)S(6)} %select_n.83), kind=kOutput, calls=%fused_computation.27 | convolution fusion | flops 134742016 | bytes 3801096 | tf_op jit(solution)/shard_map/crw,cd->drw/dot_general | solution.py:120
  77.6 3.6 %collective-permute-start.9 = (bf16[9,2,32,256]{3,2,1,0:T(8,128)(2,1)S(1)}, bf16[9,2,32,256]{3,2,1,0:T(8,128)(2,1)S(1)}, u32[]{:S(2)}, u32[]{:S(2)}) collective-permute-start(bf16[9,2,32,256]{3,2,1,0:T(8,128)(2,1)S(1)} %fusion.110), channel_id=1, source_target_pairs={{0,2},{1,3},{2,0},{3,1},{4,6},{5,7},{6,4},{7,5},{8,10},{9,11},{10,... | collective-permute-start | bytes 884744 | tf_op jit(solution)/shard_map/ppermute | solution.py:110
  83.1 5.8 %collective-permute-done.9 = bf16[9,2,32,256]{3,2,1,0:T(8,128)(2,1)S(1)} collective-permute-done((bf16[9,2,32,256]{3,2,1,0:T(8,128)(2,1)S(1)}, bf16[9,2,32,256]{3,2,1,0:T(8,128)(2,1)S(1)}, u32[]{:S(2)}, u32[]{:S(2)}) %collective-permute-start.9) | collective-permute-done | bytes 294944 | tf_op jit(solution)/shard_map/ppermute | solution.py:110
  89.0 1.8 %collective-permute-start.10 = (bf16[9,32,256]{2,1,0:T(8,128)(2,1)S(1)}, bf16[9,32,256]{2,1,0:T(8,128)(2,1)S(1)}, u32[]{:S(2)}, u32[]{:S(2)}) collective-permute-start(bf16[9,32,256]{2,1,0:T(8,128)(2,1)S(1)} %fusion.118), channel_id=1, source_target_pairs={{0,4},{1,5},{2,6},{3,7},{4,0},{5,1},{6,2},{7,3},{8,12},{9,13},{10,... | collective-permute-start | bytes 442376 | tf_op jit(solution)/shard_map/ppermute | solution.py:110
  95.4 1.5 %collective-permute-start.20 = (bf16[4,2,16,256]{3,2,0,1:T(8,128)(2,1)S(1)}, bf16[4,2,16,256]{3,2,0,1:T(8,128)(2,1)S(1)}, u32[]{:S(2)}, u32[]{:S(2)}) collective-permute-start(bf16[4,2,16,256]{3,2,0,1:T(8,128)(2,1)S(1)} %fusion.123), channel_id=1, source_target_pairs={{0,4},{1,5},{2,6},{3,7},{4,0},{5,1},{6,2},{7,3},{8,12},{9,13},{10,... | collective-permute-start | bytes 196616 | tf_op jit(solution)/shard_map/ppermute | solution.py:110
  97.0 8.3 %collective-permute-done.20 = bf16[4,2,16,256]{3,2,0,1:T(8,128)(2,1)S(1)} collective-permute-done((bf16[4,2,16,256]{3,2,0,1:T(8,128)(2,1)S(1)}, bf16[4,2,16,256]{3,2,0,1:T(8,128)(2,1)S(1)}, u32[]{:S(2)}, u32[]{:S(2)}) %collective-permute-start.20) | collective-permute-done | bytes 65568 | tf_op jit(solution)/shard_map/ppermute | solution.py:110
  105.2 1.6 %collective-permute-start.17 = (bf16[4,2,16,256]{3,2,1,0:T(8,128)(2,1)S(1)}, bf16[4,2,16,256]{3,2,1,0:T(8,128)(2,1)S(1)}, u32[]{:S(2)}, u32[]{:S(2)}) collective-permute-start(bf16[4,2,16,256]{3,2,1,0:T(8,128)(2,1)S(1)} %fusion.122), channel_id=1, source_target_pairs={{0,2},{1,3},{2,0},{3,1},{4,6},{5,7},{6,4},{7,5},{8,10},{9,11},{10,... | collective-permute-start | bytes 196616 | tf_op jit(solution)/shard_map/ppermute | solution.py:110
  106.8 2.7 %collective-permute-done.17 = bf16[4,2,16,256]{3,2,1,0:T(8,128)(2,1)S(1)} collective-permute-done((bf16[4,2,16,256]{3,2,1,0:T(8,128)(2,1)S(1)}, bf16[4,2,16,256]{3,2,1,0:T(8,128)(2,1)S(1)}, u32[]{:S(2)}, u32[]{:S(2)}) %collective-permute-start.17) | collective-permute-done | bytes 65568 | tf_op jit(solution)/shard_map/ppermute | solution.py:110
  109.5 1.6 %collective-permute-start.21 = (bf16[4,16,256]{2,1,0:T(8,128)(2,1)S(1)}, bf16[4,16,256]{2,1,0:T(8,128)(2,1)S(1)}, u32[]{:S(2)}, u32[]{:S(2)}) collective-permute-start(bf16[4,16,256]{2,1,0:T(8,128)(2,1)S(1)} %fusion.125), channel_id=1, source_target_pairs={{0,2},{1,3},{2,0},{3,1},{4,6},{5,7},{6,4},{7,5},{8,10},{9,11},{10,... | collective-permute-start | bytes 98312 | tf_op jit(solution)/shard_map/ppermute | solution.py:110
  111.1 2.4 %collective-permute-done.21 = bf16[4,16,256]{2,1,0:T(8,128)(2,1)S(1)} collective-permute-done((bf16[4,16,256]{2,1,0:T(8,128)(2,1)S(1)}, bf16[4,16,256]{2,1,0:T(8,128)(2,1)S(1)}, u32[]{:S(2)}, u32[]{:S(2)}) %collective-permute-start.21) | collective-permute-done | bytes 32800 | tf_op jit(solution)/shard_map/ppermute | solution.py:110
  113.9 1.8 %collective-permute-start.13 = (bf16[9,32,256]{2,1,0:T(8,128)(2,1)S(1)}, bf16[9,32,256]{2,1,0:T(8,128)(2,1)S(1)}, u32[]{:S(2)}, u32[]{:S(2)}) collective-permute-start(bf16[9,32,256]{2,1,0:T(8,128)(2,1)S(1)} %fusion.119), channel_id=1, source_target_pairs={{0,2},{1,3},{2,0},{3,1},{4,6},{5,7},{6,4},{7,5},{8,10},{9,11},{10,... | collective-permute-start | bytes 442376 | tf_op jit(solution)/shard_map/ppermute | solution.py:110
  115.6 1.8 %collective-permute-done.18 = bf16[4,16,256]{2,1,0:T(8,128)(2,1)S(1)} collective-permute-done((bf16[4,16,256]{2,1,0:T(8,128)(2,1)S(1)}, bf16[4,16,256]{2,1,0:T(8,128)(2,1)S(1)}, u32[]{:S(2)}, u32[]{:S(2)}) %collective-permute-start.18) | collective-permute-done | bytes 32800 | tf_op jit(solution)/shard_map/ppermute | solution.py:110
  117.4 1.6 %collective-permute-done.13 = bf16[9,32,256]{2,1,0:T(8,128)(2,1)S(1)} collective-permute-done((bf16[9,32,256]{2,1,0:T(8,128)(2,1)S(1)}, bf16[9,32,256]{2,1,0:T(8,128)(2,1)S(1)}, u32[]{:S(2)}, u32[]{:S(2)}) %collective-permute-start.13) | collective-permute-done | bytes 147488 | tf_op jit(solution)/shard_map/ppermute | solution.py:110
  119.8 2.7 %collective-permute-start.14 = (bf16[9,32,256]{2,1,0:T(8,128)(2,1)}, bf16[9,32,256]{2,1,0:T(8,128)(2,1)}, u32[]{:S(2)}, u32[]{:S(2)}) collective-permute-start(bf16[9,32,256]{2,1,0:T(8,128)(2,1)} %select_convert_fusion), channel_id=1, source_target_pairs={{0,8},{1,9},{2,10},{3,11},{4,12},{5,13},{6,14},{7,15},{8,0},{9,1},... | collective-permute-start | bytes 442376 | tf_op jit(solution)/shard_map/ppermute | solution.py:110
  125.0 1.7 %copy.244 = bf16[128,16,256]{2,1,0:T(8,128)(2,1)} copy(bf16[128,16,256]{0,2,1:T(8,128)(2,1)S(1)} %bitcast.336) | data formatting | bytes 2097152
  126.7 1.7 %collective-permute-done.23 = bf16[4,16,256]{2,1,0:T(8,128)(2,1)} collective-permute-done((bf16[4,16,256]{2,1,0:T(8,128)(2,1)}, bf16[4,16,256]{2,1,0:T(8,128)(2,1)}, u32[]{:S(2)}, u32[]{:S(2)}) %collective-permute-start.23) | collective-permute-done | bytes 32800 | tf_op jit(solution)/shard_map/ppermute | solution.py:110
  129.9 2.0 %add_multiply_fusion.1 = f32[9,32,256]{2,1,0:T(8,128)} fusion(bf16[9,32,256]{2,1,0:T(8,128)(2,1)} %collective-permute-done.14, bf16[9,32,256]{2,1,0:T(8,128)(2,1)S(1)} %collective-permute-done.10, f32[9,2,32,256]{3,2,1,0:T(8,128)} %copy-done.7, s32[]{:T(128)S(6)} %select_n.89, bf16[9,32,256]{2,1,0:T(8,128)(2,1)} %copy-done.16, ...), kind=kLoop, calls=%fused_computation.167 | loop fusion | flops 589824 | bytes 1327113 | tf_op jit(solution)/shard_map/mul | solution.py:225
  (183 shorter events, 45.3 us)
Async XLA Ops:
  0.6 16.3 %copy-start = (bf16[3,3,512,256]{3,2,1,0:T(8,128)(2,1)S(1)}, bf16[3,3,512,256]{3,2,1,0:T(8,128)(2,1)}, u32[]{:S(2)}) copy-start(bf16[3,3,512,256]{3,2,1,0:T(8,128)(2,1)} %param.6) | copy-start | bytes 7077892
  3.6 22.8 %copy-start.2 = (bf16[256,8,128]{2,0,1:T(8,128)(2,1)}, bf16[256,8,128]{2,0,1:T(8,128)(2,1)S(1)}, u32[]{:S(2)}) copy-start(bf16[256,8,128]{2,0,1:T(8,128)(2,1)S(1)} %copy.136) | copy-start | bytes 1572868
  4.3 11.9 %collective-permute-start.6 = (bf16[256,1,128]{2,0,1:T(8,128)(2,1)}, bf16[256,1,128]{2,0,1:T(8,128)(2,1)S(1)}, u32[]{:S(2)}, u32[]{:S(2)}) collective-permute-start(bf16[256,1,128]{2,0,1:T(8,128)(2,1)} %get-tuple-element.31), channel_id=1, source_target_pairs={{1,0},{2,1},{3,2},{4,3},{5,4},{6,5},{7,6},{8,7},{9,8},{10,9},{11,1... | collective-permute-start | bytes 196616 | tf_op jit(solution)/shard_map/ppermute | solution.py:164
  5.6 10.7 %collective-permute-start.5 = (bf16[256,1,128]{2,0,1:T(8,128)(2,1)}, bf16[256,1,128]{2,0,1:T(8,128)(2,1)S(1)}, u32[]{:S(2)}, u32[]{:S(2)}) collective-permute-start(bf16[256,1,128]{2,0,1:T(8,128)(2,1)} %get-tuple-element.30), channel_id=1, source_target_pairs={{0,1},{1,2},{2,3},{3,4},{4,5},{5,6},{6,7},{7,8},{8,9},{9,10},{10,1... | collective-permute-start | bytes 196616 | tf_op jit(solution)/shard_map/ppermute | solution.py:163
  8.6 26.8 %collective-permute-start = (bf16[16,256,128]{2,1,0:T(8,128)(2,1)}, bf16[16,256,128]{2,1,0:T(8,128)(2,1)}, u32[]{:S(2)}, u32[]{:S(2)}) collective-permute-start(bf16[16,256,128]{2,1,0:T(8,128)(2,1)} %bitcast.333), channel_id=1, source_target_pairs={{0,16},{16,0},{1,17},{17,1},{2,18},{18,2},{3,19},{19,3},{4,20},{20... | collective-permute-start | bytes 3145736 | tf_op jit(solution)/shard_map/ppermute | solution.py:110
  16.2 19.2 %copy-start.14 = (bf16[2,2,128,256]{3,2,1,0:T(8,128)(2,1)}, bf16[2,2,128,256]{3,2,1,0:T(8,128)(2,1)S(1)}, u32[]{:S(2)}) copy-start(bf16[2,2,128,256]{3,2,1,0:T(8,128)(2,1)S(1)} %constant_dynamic-slice_fusion.4) | copy-start | bytes 786436
  16.3 10.1 %copy-start.17 = (bf16[256,1,128]{2,0,1:T(8,128)(2,1)}, bf16[256,1,128]{2,0,1:T(8,128)(2,1)S(1)}, u32[]{:S(2)}) copy-start(bf16[256,1,128]{2,0,1:T(8,128)(2,1)S(1)} %collective-permute-done.5) | copy-start | bytes 196612
  38.1 25.2 %collective-permute-start.4 = (bf16[256,8,128]{0,2,1:T(8,128)(2,1)S(1)}, bf16[256,8,128]{0,2,1:T(8,128)(2,1)}, u32[]{:S(2)}, u32[]{:S(2)}) collective-permute-start(bf16[256,8,128]{0,2,1:T(8,128)(2,1)S(1)} %get-tuple-element.34), channel_id=1, source_target_pairs={{0,16},{16,0},{1,17},{17,1},{2,18},{18,2},{3,19},{19,3},{4,20},{20... | collective-permute-start | bytes 1572872 | tf_op jit(solution)/shard_map/ppermute | solution.py:110
  41.2 21.2 %collective-permute-start.3 = (bf16[256,1,128]{0,2,1:T(8,128)(2,1)}, bf16[256,1,128]{0,2,1:T(8,128)(2,1)}, u32[]{:S(2)}, u32[]{:S(2)}) collective-permute-start(bf16[256,1,128]{0,2,1:T(8,128)(2,1)} %get-tuple-element.32), channel_id=1, source_target_pairs={{0,17},{1,18},{2,19},{3,20},{4,21},{5,22},{6,23},{7,24},{8,25},{9,... | collective-permute-start | bytes 196616 | tf_op jit(solution)/shard_map/ppermute | solution.py:163
  43.4 8.6 %collective-permute-start.1 = (bf16[256,1,128]{0,2,1:T(8,128)(2,1)}, bf16[256,1,128]{0,2,1:T(8,128)(2,1)S(1)}, u32[]{:S(2)}, u32[]{:S(2)}) collective-permute-start(bf16[256,1,128]{0,2,1:T(8,128)(2,1)} %get-tuple-element.32), channel_id=1, source_target_pairs={{0,1},{1,2},{2,3},{3,4},{4,5},{5,6},{6,7},{7,8},{8,9},{9,10},{10,1... | collective-permute-start | bytes 196616 | tf_op jit(solution)/shard_map/ppermute | solution.py:163
  45.7 17.6 %collective-permute-start.7 = (bf16[256,1,128]{0,2,1:T(8,128)(2,1)}, bf16[256,1,128]{0,2,1:T(8,128)(2,1)}, u32[]{:S(2)}, u32[]{:S(2)}) collective-permute-start(bf16[256,1,128]{0,2,1:T(8,128)(2,1)} %get-tuple-element.33), channel_id=1, source_target_pairs={{1,16},{2,17},{3,18},{4,19},{5,20},{6,21},{7,22},{8,23},{9,24},{10... | collective-permute-start | bytes 196616 | tf_op jit(solution)/shard_map/ppermute | solution.py:164
  47.0 5.1 %collective-permute-start.2 = (bf16[256,1,128]{0,2,1:T(8,128)(2,1)}, bf16[256,1,128]{0,2,1:T(8,128)(2,1)S(1)}, u32[]{:S(2)}, u32[]{:S(2)}) collective-permute-start(bf16[256,1,128]{0,2,1:T(8,128)(2,1)} %get-tuple-element.33), channel_id=1, source_target_pairs={{1,0},{2,1},{3,2},{4,3},{5,4},{6,5},{7,6},{8,7},{9,8},{10,9},{11,1... | collective-permute-start | bytes 196616 | tf_op jit(solution)/shard_map/ppermute | solution.py:164
  56.1 21.2 %collective-permute-start.8 = (bf16[9,2,2,32,256]{4,3,2,1,0:T(8,128)(2,1)S(1)}, bf16[9,2,2,32,256]{4,3,2,1,0:T(8,128)(2,1)S(1)}, u32[]{:S(2)}, u32[]{:S(2)}) collective-permute-start(bf16[9,2,2,32,256]{4,3,2,1,0:T(8,128)(2,1)S(1)} %fusion.30), channel_id=1, source_target_pairs={{0,1},{1,0},{2,3},{3,2},{4,5},{5,4},{6,7},{7,6},{8,9},{9,8},{10,11... | collective-permute-start | bytes 1769480 | tf_op jit(solution)/shard_map/ppermute | solution.py:110
  70.7 20.1 %collective-permute-start.15 = (bf16[256,8,128]{0,2,1:T(8,128)(2,1)S(1)}, bf16[256,8,128]{0,2,1:T(8,128)(2,1)S(1)}, u32[]{:S(2)}, u32[]{:S(2)}) collective-permute-start(bf16[256,8,128]{0,2,1:T(8,128)(2,1)S(1)} %copy-done.21), channel_id=1, source_target_pairs={{0,16},{16,0},{1,17},{17,1},{2,18},{18,2},{3,19},{19,3},{4,20},{20... | collective-permute-start | bytes 1572872 | tf_op jit(solution)/shard_map/ppermute | solution.py:110
  71.8 51.6 %collective-permute-start.24 = (bf16[2,2,128,256]{3,2,1,0:T(8,128)(2,1)S(1)}, bf16[2,2,128,256]{3,2,1,0:T(8,128)(2,1)S(1)}, u32[]{:S(2)}, u32[]{:S(2)}) collective-permute-start(bf16[2,2,128,256]{3,2,1,0:T(8,128)(2,1)S(1)} %copy-done.15), channel_id=1, source_target_pairs={{0,16},{16,0},{1,17},{17,1},{2,18},{18,2},{3,19},{19,3},{4,20},{20... | collective-permute-start | bytes 786440 | tf_op jit(solution)/shard_map/ppermute | solution.py:110
  74.4 19.6 %collective-permute-start.11 = (bf16[9,2,2,32,256]{4,3,0,2,1:T(8,128)(2,1)S(1)}, bf16[9,2,2,32,256]{4,3,0,2,1:T(8,128)(2,1)S(1)}, u32[]{:S(2)}, u32[]{:S(2)}) collective-permute-start(bf16[9,2,2,32,256]{4,3,0,2,1:T(8,128)(2,1)S(1)} %fusion.31), channel_id=1, source_target_pairs={{0,1},{1,0},{2,3},{3,2},{4,5},{5,4},{6,7},{7,6},{8,9},{9,8},{10,11... | collective-permute-start | bytes 1769480 | tf_op jit(solution)/shard_map/ppermute | solution.py:110
  77.6 11.3 %collective-permute-start.9 = (bf16[9,2,32,256]{3,2,1,0:T(8,128)(2,1)S(1)}, bf16[9,2,32,256]{3,2,1,0:T(8,128)(2,1)S(1)}, u32[]{:S(2)}, u32[]{:S(2)}) collective-permute-start(bf16[9,2,32,256]{3,2,1,0:T(8,128)(2,1)S(1)} %fusion.110), channel_id=1, source_target_pairs={{0,2},{1,3},{2,0},{3,1},{4,6},{5,7},{6,4},{7,5},{8,10},{9,11},{10,... | collective-permute-start | bytes 884744 | tf_op jit(solution)/shard_map/ppermute | solution.py:110
  81.2 9.6 %copy-start.6 = (f32[256,8,128]{0,2,1:T(8,128)S(1)}, f32[256,8,128]{0,2,1:T(8,128)}, u32[]{:S(2)}) copy-start(f32[256,8,128]{0,2,1:T(8,128)} %get-tuple-element.35) | copy-start | bytes 3145732
  88.9 30.1 %copy-start.7 = (f32[9,2,32,256]{3,2,1,0:T(8,128)}, f32[9,2,32,256]{3,2,1,0:T(8,128)S(1)}, u32[]{:S(2)}) copy-start(f32[9,2,32,256]{3,2,1,0:T(8,128)S(1)} %bitcast_add_fusion.2) | copy-start | bytes 1769476
  89.0 28.5 %collective-permute-start.10 = (bf16[9,32,256]{2,1,0:T(8,128)(2,1)S(1)}, bf16[9,32,256]{2,1,0:T(8,128)(2,1)S(1)}, u32[]{:S(2)}, u32[]{:S(2)}) collective-permute-start(bf16[9,32,256]{2,1,0:T(8,128)(2,1)S(1)} %fusion.118), channel_id=1, source_target_pairs={{0,4},{1,5},{2,6},{3,7},{4,0},{5,1},{6,2},{7,3},{8,12},{9,13},{10,... | collective-permute-start | bytes 442376 | tf_op jit(solution)/shard_map/ppermute | solution.py:110
  91.7 30.9 %collective-permute-start.22 = (bf16[256,8,128]{0,2,1:T(8,128)(2,1)S(1)}, bf16[256,8,128]{0,2,1:T(8,128)(2,1)S(1)}, u32[]{:S(2)}, u32[]{:S(2)}) collective-permute-start(bf16[256,8,128]{0,2,1:T(8,128)(2,1)S(1)} %fusion.18), channel_id=1, source_target_pairs={{0,16},{16,0},{1,17},{17,1},{2,18},{18,2},{3,19},{19,3},{4,20},{20... | collective-permute-start | bytes 1572872 | tf_op jit(solution)/shard_map/ppermute | solution.py:110
  92.7 1.9 %collective-permute-start.19 = (bf16[4,2,2,16,256]{4,3,0,2,1:T(8,128)(2,1)S(1)}, bf16[4,2,2,16,256]{4,3,0,2,1:T(8,128)(2,1)S(1)}, u32[]{:S(2)}, u32[]{:S(2)}) collective-permute-start(bf16[4,2,2,16,256]{4,3,0,2,1:T(8,128)(2,1)S(1)} %fusion.121), channel_id=1, source_target_pairs={{0,1},{1,0},{2,3},{3,2},{4,5},{5,4},{6,7},{7,6},{8,9},{9,8},{10,11... | collective-permute-start | bytes 393224 | tf_op jit(solution)/shard_map/ppermute | solution.py:110
  93.9 1.4 %collective-permute-start.16 = (bf16[4,2,2,16,256]{4,3,2,1,0:T(8,128)(2,1)S(1)}, bf16[4,2,2,16,256]{4,3,2,1,0:T(8,128)(2,1)S(1)}, u32[]{:S(2)}, u32[]{:S(2)}) collective-permute-start(bf16[4,2,2,16,256]{4,3,2,1,0:T(8,128)(2,1)S(1)} %fusion.120), channel_id=1, source_target_pairs={{0,1},{1,0},{2,3},{3,2},{4,5},{5,4},{6,7},{7,6},{8,9},{9,8},{10,11... | collective-permute-start | bytes 393224 | tf_op jit(solution)/shard_map/ppermute | solution.py:110
  94.7 19.1 %collective-permute-start.12 = (bf16[9,2,32,256]{3,2,0,1:T(8,128)(2,1)S(1)}, bf16[9,2,32,256]{3,2,0,1:T(8,128)(2,1)S(1)}, u32[]{:S(2)}, u32[]{:S(2)}) collective-permute-start(bf16[9,2,32,256]{3,2,0,1:T(8,128)(2,1)S(1)} %fusion.111), channel_id=1, source_target_pairs={{0,4},{1,5},{2,6},{3,7},{4,0},{5,1},{6,2},{7,3},{8,12},{9,13},{10,... | collective-permute-start | bytes 884744 | tf_op jit(solution)/shard_map/ppermute | solution.py:110
  95.4 9.9 %collective-permute-start.20 = (bf16[4,2,16,256]{3,2,0,1:T(8,128)(2,1)S(1)}, bf16[4,2,16,256]{3,2,0,1:T(8,128)(2,1)S(1)}, u32[]{:S(2)}, u32[]{:S(2)}) collective-permute-start(bf16[4,2,16,256]{3,2,0,1:T(8,128)(2,1)S(1)} %fusion.123), channel_id=1, source_target_pairs={{0,4},{1,5},{2,6},{3,7},{4,0},{5,1},{6,2},{7,3},{8,12},{9,13},{10,... | collective-permute-start | bytes 196616 | tf_op jit(solution)/shard_map/ppermute | solution.py:110
  105.2 4.3 %collective-permute-start.17 = (bf16[4,2,16,256]{3,2,1,0:T(8,128)(2,1)S(1)}, bf16[4,2,16,256]{3,2,1,0:T(8,128)(2,1)S(1)}, u32[]{:S(2)}, u32[]{:S(2)}) collective-permute-start(bf16[4,2,16,256]{3,2,1,0:T(8,128)(2,1)S(1)} %fusion.122), channel_id=1, source_target_pairs={{0,2},{1,3},{2,0},{3,1},{4,6},{5,7},{6,4},{7,5},{8,10},{9,11},{10,... | collective-permute-start | bytes 196616 | tf_op jit(solution)/shard_map/ppermute | solution.py:110
  109.5 4.0 %collective-permute-start.21 = (bf16[4,16,256]{2,1,0:T(8,128)(2,1)S(1)}, bf16[4,16,256]{2,1,0:T(8,128)(2,1)S(1)}, u32[]{:S(2)}, u32[]{:S(2)}) collective-permute-start(bf16[4,16,256]{2,1,0:T(8,128)(2,1)S(1)} %fusion.125), channel_id=1, source_target_pairs={{0,2},{1,3},{2,0},{3,1},{4,6},{5,7},{6,4},{7,5},{8,10},{9,11},{10,... | collective-permute-start | bytes 98312 | tf_op jit(solution)/shard_map/ppermute | solution.py:110
  113.5 3.9 %collective-permute-start.18 = (bf16[4,16,256]{2,1,0:T(8,128)(2,1)S(1)}, bf16[4,16,256]{2,1,0:T(8,128)(2,1)S(1)}, u32[]{:S(2)}, u32[]{:S(2)}) collective-permute-start(bf16[4,16,256]{2,1,0:T(8,128)(2,1)S(1)} %fusion.124), channel_id=1, source_target_pairs={{0,4},{1,5},{2,6},{3,7},{4,0},{5,1},{6,2},{7,3},{8,12},{9,13},{10,... | collective-permute-start | bytes 98312 | tf_op jit(solution)/shard_map/ppermute | solution.py:110
  113.7 9.7 %copy-start.19 = (f32[4,16,256]{2,1,0:T(8,128)}, f32[4,16,256]{2,1,0:T(8,128)S(1)}, u32[]{:S(2)}) copy-start(f32[4,16,256]{2,1,0:T(8,128)S(1)} %bitcast_add_fusion.9) | copy-start | bytes 196612
  113.9 5.2 %collective-permute-start.13 = (bf16[9,32,256]{2,1,0:T(8,128)(2,1)S(1)}, bf16[9,32,256]{2,1,0:T(8,128)(2,1)S(1)}, u32[]{:S(2)}, u32[]{:S(2)}) collective-permute-start(bf16[9,32,256]{2,1,0:T(8,128)(2,1)S(1)} %fusion.119), channel_id=1, source_target_pairs={{0,2},{1,3},{2,0},{3,1},{4,6},{5,7},{6,4},{7,5},{8,10},{9,11},{10,... | collective-permute-start | bytes 442376 | tf_op jit(solution)/shard_map/ppermute | solution.py:110
  119.8 10.1 %collective-permute-start.14 = (bf16[9,32,256]{2,1,0:T(8,128)(2,1)}, bf16[9,32,256]{2,1,0:T(8,128)(2,1)}, u32[]{:S(2)}, u32[]{:S(2)}) collective-permute-start(bf16[9,32,256]{2,1,0:T(8,128)(2,1)} %select_convert_fusion), channel_id=1, source_target_pairs={{0,8},{1,9},{2,10},{3,11},{4,12},{5,13},{6,14},{7,15},{8,0},{9,1},... | collective-permute-start | bytes 442376 | tf_op jit(solution)/shard_map/ppermute | solution.py:110
  123.2 5.1 %collective-permute-start.23 = (bf16[4,16,256]{2,1,0:T(8,128)(2,1)}, bf16[4,16,256]{2,1,0:T(8,128)(2,1)}, u32[]{:S(2)}, u32[]{:S(2)}) collective-permute-start(bf16[4,16,256]{2,1,0:T(8,128)(2,1)} %select_convert_fusion.1), channel_id=1, source_target_pairs={{0,8},{1,9},{2,10},{3,11},{4,12},{5,13},{6,14},{7,15},{8,0},{9,1},... | collective-permute-start | bytes 98312 | tf_op jit(solution)/shard_map/ppermute | solution.py:110
  (15 other events, 68.4 us)

commit v3 on v2

--- a/solution.py
+++ b/solution.py
@@ -200,9 +200,10 @@
     preact = preact + jnp.einsum("rawbc,abcd->drw", far, down_far, preferred_element_type=f32)
     cdf = normal_cdf(preact)
     hidden = (preact * cdf).astype(bf16)
+    hidden, away = lax.optimization_barrier((hidden, away))
     hidden_far = flip(hidden, "chan", 1)
     own_edges, far_edges = edge_rows(hidden, False), edge_rows(hidden, True)
-    hidden_far, away, down_far = lax.optimization_barrier((hidden_far, away, down_far))
+    hidden_far, down_far = lax.optimization_barrier((hidden_far, down_far))
     got = flip(away, "chan", 1)
     down_back = flip(down_far, "chan", 1)
 

time: 133 us -> 138 us (1.038)
  waiting for transfers between devices: 32.5 us -> 24.6 us
  local copies, waits for them, and re-layouts: 18.6 us -> 25.9 us
  other arithmetic: 7.12 us -> 9.3 us
  starting transfers between devices: 38.5 us -> 40.6 us
  matrix products: 33.5 us -> 35.1 us
    ppermute x19, waiting for transfers between devices: 32.3 us -> 24.6 us  [flip(): return lax.ppermute(block, axis, [(i, i ^ mask) for i in range(count)])]
    ppermute x3, starting transfers between devices: 7.53 us -> 13.3 us  [edge_rows(): low = lax.ppermute(block[:, -1:], ('chan', 'tile'), down)]
    ppermute x19, starting transfers between devices: 27.1 us -> 23.5 us  [flip(): return lax.ppermute(block, axis, [(i, i ^ mask) for i in range(count)])]
    unnamed x66 -> x58, local copies, waits for them, and re-layouts: 9.34 us -> 11.9 us
    concatenate x3, other arithmetic: 2.12 us -> 4.07 us  [rimmed(): jnp.concatenate([low, block, high], axis=1)]
    optimization_barrier x0 -> x1, local copies, waits for them, and re-layouts: none -> 1.81 us  [pair_device(): hidden_far, down_far = lax.optimization_barrier((hidden_far, down_far))]
    convert_element_type x12, local copies, waits for them, and re-layouts: 0.44 us -> 1.83 us  [halve(): got = flip(send.astype(jnp.bfloat16), 'tile', 1 << bit)]
  transfers between devices with their start and end apart: 25 -> 25, of which waited for: 10 -> 8; matrix products, arithmetic and copies ran while one was open for 38% -> 43% of each run, Pallas kernels for 0% -> 0%
where the time goes in v3:
time: 138 us; the launch traced here: 137 us
  starting transfers between devices  40.6 us (29%)
  matrix products  35.1 us (25%)
  local copies, waits for them, and re-layouts  25.9 us (19%)
  waiting for transfers between devices  24.6 us (18%)
  other arithmetic  9.3 us (7%)
  between operations  1.64 us (1%)
    ppermute x19, waiting for transfers between devices, flip(): return lax.ppermute(block, axis, [(i, i ^ mask) for i in range(count)])  24.6 us
    ppermute x19, starting transfers between devices, flip(): return lax.ppermute(block, axis, [(i, i ^ mask) for i in range(count)])  23.5 us
    dot_general x36, matrix products, tap_sum(): jnp.einsum(form, window, weights[i, j], preferred_element_type=jnp.float32)  18.2 us
    ppermute x3, starting transfers between devices, edge_rows(): low = lax.ppermute(block[:, -1:], ('chan', 'tile'), down)  13.3 us
    unnamed x58, local copies, waits for them, and re-layouts  11.9 us
    dot_general x18, matrix products, mix_terms(): jnp.einsum('crw,drw->cd', window, cotangent, preferred_element_type=f32)  9.21 us
    dot_general x2, local copies, waits for them, and re-layouts, down_terms(): jnp.einsum('rawbc,drw->abcd', patches, grad_pre, preferred_element_type=f32)  5.37 us
    concatenate x3, other arithmetic, rimmed(): jnp.concatenate([low, block, high], axis=1)  4.07 us
  transfers between devices with their start and end apart: 25, of which 8 were waited for; matrix products, arithmetic and copies ran while one was open for 43% of the time, Pallas kernels for 0%

profile of v3, /device:TPU:0, one launch (start us, length us, event | category | flops | bytes accessed | tf_op | source)
XLA Modules:
  0.0 137.1 jit_solution(1440696138190637073)
XLA Ops:
  0.7 2.8 %copy.75 = bf16[128,16,256]{0,2,1:T(8,128)(2,1)} copy(bf16[128,16,256]{2,1,0:T(8,128)(2,1)} %param.4) | data formatting | bytes 2097152 | tf_op args[0]
  4.2 2.3 %collective-permute-start.1 = (bf16[256,1,128]{2,0,1:T(8,128)(2,1)}, bf16[256,1,128]{2,0,1:T(8,128)(2,1)S(1)}, u32[]{:S(2)}, u32[]{:S(2)}) collective-permute-start(bf16[256,1,128]{2,0,1:T(8,128)(2,1)} %get-tuple-element.36), channel_id=1, source_target_pairs={{0,1},{1,2},{2,3},{3,4},{4,5},{5,6},{6,7},{7,8},{8,9},{9,10},{10,1... | collective-permute-start | bytes 196616 | tf_op jit(solution)/shard_map/ppermute | solution.py:163
  7.9 2.4 %collective-permute-start = (bf16[16,256,128]{2,1,0:T(8,128)(2,1)}, bf16[16,256,128]{2,1,0:T(8,128)(2,1)}, u32[]{:S(2)}, u32[]{:S(2)}) collective-permute-start(bf16[16,256,128]{2,1,0:T(8,128)(2,1)} %bitcast.336), channel_id=1, source_target_pairs={{0,16},{16,0},{1,17},{17,1},{2,18},{18,2},{3,19},{19,3},{4,20},{20... | collective-permute-start | bytes 3145736 | tf_op jit(solution)/shard_map/ppermute | solution.py:110
  10.3 2.9 %convolution_bitcast_fusion.1 = f32[256,8,128]{2,0,1:T(8,128)} fusion(bf16[8,2,128,2,128]{4,3,2,1,0:T(2,128)(2,1)} %bitcast.337, bf16[2,2,256,256]{3,2,1,0:T(8,128)(2,1)} %param.5, s32[]{:T(128)S(6)} %select_n.81), kind=kOutput, calls=%fused_computation.42 | convolution fusion | flops 268435456 | bytes 2359300 | tf_op jit(solution)/shard_map/rawbc,abcd->drw/dot_general | solution.py:199
  13.9 1.8 %copy.206 = bf16[2,2,128,256]{2,3,1,0:T(8,128)(2,1)} copy(bf16[2,2,128,256]{3,2,1,0:T(8,128)(2,1)} %constant_dynamic-slice_fusion.4) | data formatting | bytes 524288 | tf_op jit(solution)/shard_map/optimization_barrier | solution.py:206
  15.7 2.7 %copy.121 = bf16[2,2,128,8,128]{4,3,2,1,0:T(8,128)(2,1)} copy(bf16[2,2,128,8,128]{2,1,4,0,3:T(2,128)(2,1)} %bitcast.338) | data formatting | bytes 2097152 | tf_op jit(solution)/shard_map/rawbc,drw->abcd/dot_general | solution.py:232
  22.5 1.4 %convolution_add_fusion.1 = f32[256,8,128]{2,0,1:T(8,128)} fusion(f32[256,8,128]{2,0,1:T(8,128)S(1)} %convolution_add_fusion.2, bf16[256,10,130]{2,0,1:T(8,128)(2,1)S(1)} %fusion.14, bf16[3,3,512,256]{3,2,1,0:T(8,128)(2,1)S(1)} %copy-done, s32[]{:T(128)S(6)} %add.289, s32[]{:T(128)S(6)} %select_n.80), kind=kOutput, calls=%fused_computation.10 | convolution fusion | flops 134479872 | bytes 2752520 | tf_op jit(solution)/shard_map/drw,cd->crw/dot_general | solution.py:120
  27.8 4.8 %collective-permute-done = bf16[16,256,128]{2,1,0:T(8,128)(2,1)} collective-permute-done((bf16[16,256,128]{2,1,0:T(8,128)(2,1)}, bf16[16,256,128]{2,1,0:T(8,128)(2,1)}, u32[]{:S(2)}, u32[]{:S(2)}) %collective-permute-start) | collective-permute-done | bytes 1048608 | tf_op jit(solution)/shard_map/ppermute | solution.py:110
  32.7 2.9 %multiply_convert_fusion = (bf16[256,8,128]{2,0,1:T(8,128)(2,1)}, f32[256,8,128]{2,0,1:T(8,128)}) fusion(f32[256,8,128]{2,0,1:T(8,128)S(1)} %copy-done.3, bf16[8,2,128,2,128]{4,3,2,1,0:T(2,128)(2,1)} %bitcast.10, bf16[2,2,128,256]{3,2,1,0:T(8,128)(2,1)S(1)} %copy-done.8), kind=kOutput, calls=%fused_computation.71 | convolution fusion | flops 270008320 | bytes 3932160 | tf_op jit(solution)/shard_map/rawbc,abcd->drw/dot_general | solution.py:200
  35.6 1.5 %fusion.180 = (bf16[256,1,128]{2,0,1:T(8,128)(2,1)}, bf16[256,1,128]{2,0,1:T(8,128)(2,1)}) fusion(bf16[256,8,128]{2,0,1:T(8,128)(2,1)} %get-tuple-element.15), kind=kLoop, calls=%fused_computation.300 | loop fusion | bytes 262144 | tf_op jit(solution)/shard_map/slice | solution.py:163
  37.1 5.9 %collective-permute-start.5 = (bf16[256,1,128]{2,0,1:T(8,128)(2,1)}, bf16[256,1,128]{2,0,1:T(8,128)(2,1)}, u32[]{:S(2)}, u32[]{:S(2)}) collective-permute-start(bf16[256,1,128]{2,0,1:T(8,128)(2,1)} %get-tuple-element.34), channel_id=1, source_target_pairs={{0,17},{1,18},{2,19},{3,20},{4,21},{5,22},{6,23},{7,24},{8,25},{9,... | collective-permute-start | bytes 196616 | tf_op jit(solution)/shard_map/ppermute | solution.py:163
  43.0 5.0 %collective-permute-start.3 = (bf16[256,1,128]{2,0,1:T(8,128)(2,1)}, bf16[256,1,128]{2,0,1:T(8,128)(2,1)}, u32[]{:S(2)}, u32[]{:S(2)}) collective-permute-start(bf16[256,1,128]{2,0,1:T(8,128)(2,1)} %get-tuple-element.34), channel_id=1, source_target_pairs={{0,1},{1,2},{2,3},{3,4},{4,5},{5,6},{6,7},{7,8},{8,9},{9,10},{10,1... | collective-permute-start | bytes 196616 | tf_op jit(solution)/shard_map/ppermute | solution.py:163
  50.6 2.1 %fusion.172 = f32[256,256,1]{1,0,2:T(8,128)} fusion(bf16[256,8,128]{2,0,1:T(8,128)(2,1)} %get-tuple-element.15, bf16[256,8,128]{2,1,0:T(8,128)(2,1)S(1)} %copy-done.1), kind=kOutput, calls=%fused_computation.292 | convolution fusion | flops 134217728 | bytes 1310720 | tf_op jit(solution)/shard_map/crw,drw->cd/dot_general | solution.py:220
  53.2 2.7 %copy.133 = bf16[2,2,128,8,128]{4,3,2,1,0:T(8,128)(2,1)} copy(bf16[2,2,128,8,128]{2,1,4,0,3:T(2,128)(2,1)} %bitcast.136) | data formatting | bytes 2097152 | tf_op jit(solution)/shard_map/rawbc,drw->abcd/dot_general | solution.py:232
  55.9 1.5 %collective-permute-start.15 = (bf16[256,8,128]{2,0,1:T(8,128)(2,1)}, bf16[256,8,128]{2,0,1:T(8,128)(2,1)S(1)}, u32[]{:S(2)}, u32[]{:S(2)}) collective-permute-start(bf16[256,8,128]{2,0,1:T(8,128)(2,1)} %fusion.16), channel_id=1, source_target_pairs={{0,16},{16,0},{1,17},{17,1},{2,18},{18,2},{3,19},{19,3},{4,20},{20... | collective-permute-start | bytes 1572872 | tf_op jit(solution)/shard_map/ppermute | solution.py:110
  60.2 1.7 %select_maximum_fusion.2 = bf16[256,10,130]{2,0,1:T(8,128)(2,1)S(1)} fusion(bf16[256,1,128]{2,0,1:T(8,128)(2,1)} %collective-permute-done.4, bf16[256,8,128]{2,0,1:T(8,128)(2,1)} %get-tuple-element.15, bf16[256,1,128]{2,0,1:T(8,128)(2,1)} %collective-permute-done.3), kind=kLoop, calls=%fused_computation.45 | loop fusion | flops 3993600 | bytes 1320960 | tf_op jit(solution)/shard_map/concatenate | solution.py:170
  69.5 1.4 %collective-permute-start.8 = (bf16[9,2,2,32,256]{4,3,2,1,0:T(8,128)(2,1)S(1)}, bf16[9,2,2,32,256]{4,3,2,1,0:T(8,128)(2,1)S(1)}, u32[]{:S(2)}, u32[]{:S(2)}) collective-permute-start(bf16[9,2,2,32,256]{4,3,2,1,0:T(8,128)(2,1)S(1)} %fusion.28), channel_id=1, source_target_pairs={{0,1},{1,0},{2,3},{3,2},{4,5},{5,4},{6,7},{7,6},{8,9},{9,8},{10,11... | collective-permute-start | bytes 1769480 | tf_op jit(solution)/shard_map/ppermute | solution.py:110
  74.0 1.7 %select_maximum_fusion = bf16[256,10,130]{2,0,1:T(8,128)(2,1)S(1)} fusion(bf16[256,1,128]{2,0,1:T(8,128)(2,1)S(1)} %collective-permute-done.7, bf16[256,8,128]{2,0,1:T(8,128)(2,1)} %collective-permute-done.6, bf16[256,1,128]{2,0,1:T(8,128)(2,1)} %collective-permute-done.5), kind=kLoop, calls=%fused_computation.43 | loop fusion | flops 3993600 | bytes 1320960 | tf_op jit(solution)/shard_map/concatenate | solution.py:170
  82.1 1.6 %collective-permute-start.22 = (bf16[256,8,128]{2,0,1:T(8,128)(2,1)S(1)}, bf16[256,8,128]{2,0,1:T(8,128)(2,1)S(1)}, u32[]{:S(2)}, u32[]{:S(2)}) collective-permute-start(bf16[256,8,128]{2,0,1:T(8,128)(2,1)S(1)} %fusion.17), channel_id=1, source_target_pairs={{0,16},{16,0},{1,17},{17,1},{2,18},{18,2},{3,19},{19,3},{4,20},{20... | collective-permute-start | bytes 1572872 | tf_op jit(solution)/shard_map/ppermute | solution.py:110
  91.9 2.8 %collective-permute-start.20 = (bf16[4,2,16,256]{3,2,0,1:T(8,128)(2,1)S(1)}, bf16[4,2,16,256]{3,2,0,1:T(8,128)(2,1)S(1)}, u32[]{:S(2)}, u32[]{:S(2)}) collective-permute-start(bf16[4,2,16,256]{3,2,0,1:T(8,128)(2,1)S(1)} %fusion.109), channel_id=1, source_target_pairs={{0,4},{1,5},{2,6},{3,7},{4,0},{5,1},{6,2},{7,3},{8,12},{9,13},{10,... | collective-permute-start | bytes 196616 | tf_op jit(solution)/shard_map/ppermute | solution.py:110
  95.7 1.6 %collective-permute-done.20 = bf16[4,2,16,256]{3,2,0,1:T(8,128)(2,1)S(1)} collective-permute-done((bf16[4,2,16,256]{3,2,0,1:T(8,128)(2,1)S(1)}, bf16[4,2,16,256]{3,2,0,1:T(8,128)(2,1)S(1)}, u32[]{:S(2)}, u32[]{:S(2)}) %collective-permute-start.20) | collective-permute-done | bytes 65568 | tf_op jit(solution)/shard_map/ppermute | solution.py:110
  97.3 1.4 %collective-permute-start.9 = (bf16[9,2,32,256]{3,2,1,0:T(8,128)(2,1)S(1)}, bf16[9,2,32,256]{3,2,1,0:T(8,128)(2,1)S(1)}, u32[]{:S(2)}, u32[]{:S(2)}) collective-permute-start(bf16[9,2,32,256]{3,2,1,0:T(8,128)(2,1)S(1)} %fusion.96), channel_id=1, source_target_pairs={{0,2},{1,3},{2,0},{3,1},{4,6},{5,7},{6,4},{7,5},{8,10},{9,11},{10,... | collective-permute-start | bytes 884744 | tf_op jit(solution)/shard_map/ppermute | solution.py:110
  99.8 6.9 %collective-permute-done.21 = bf16[4,16,256]{2,1,0:T(8,128)(2,1)S(1)} collective-permute-done((bf16[4,16,256]{2,1,0:T(8,128)(2,1)S(1)}, bf16[4,16,256]{2,1,0:T(8,128)(2,1)S(1)}, u32[]{:S(2)}, u32[]{:S(2)}) %collective-permute-start.21) | collective-permute-done | bytes 32800 | tf_op jit(solution)/shard_map/ppermute | solution.py:110
  106.7 1.5 %collective-permute-start.18 = (bf16[4,16,256]{2,1,0:T(8,128)(2,1)S(1)}, bf16[4,16,256]{2,1,0:T(8,128)(2,1)S(1)}, u32[]{:S(2)}, u32[]{:S(2)}) collective-permute-start(bf16[4,16,256]{2,1,0:T(8,128)(2,1)S(1)} %fusion.110), channel_id=1, source_target_pairs={{0,4},{1,5},{2,6},{3,7},{4,0},{5,1},{6,2},{7,3},{8,12},{9,13},{10,... | collective-permute-start | bytes 98312 | tf_op jit(solution)/shard_map/ppermute | solution.py:110
  108.2 2.4 %collective-permute-done.18 = bf16[4,16,256]{2,1,0:T(8,128)(2,1)S(1)} collective-permute-done((bf16[4,16,256]{2,1,0:T(8,128)(2,1)S(1)}, bf16[4,16,256]{2,1,0:T(8,128)(2,1)S(1)}, u32[]{:S(2)}, u32[]{:S(2)}) %collective-permute-start.18) | collective-permute-done | bytes 32800 | tf_op jit(solution)/shard_map/ppermute | solution.py:110
  111.0 1.6 %collective-permute-start.12 = (bf16[9,2,32,256]{3,2,0,1:T(8,128)(2,1)S(1)}, bf16[9,2,32,256]{3,2,0,1:T(8,128)(2,1)S(1)}, u32[]{:S(2)}, u32[]{:S(2)}) collective-permute-start(bf16[9,2,32,256]{3,2,0,1:T(8,128)(2,1)S(1)} %fusion.97), channel_id=1, source_target_pairs={{0,4},{1,5},{2,6},{3,7},{4,0},{5,1},{6,2},{7,3},{8,12},{9,13},{10,... | collective-permute-start | bytes 884744 | tf_op jit(solution)/shard_map/ppermute | solution.py:110
  114.4 2.5 %collective-permute-start.23 = (bf16[4,16,256]{2,1,0:T(8,128)(2,1)}, bf16[4,16,256]{2,1,0:T(8,128)(2,1)}, u32[]{:S(2)}, u32[]{:S(2)}) collective-permute-start(bf16[4,16,256]{2,1,0:T(8,128)(2,1)} %select_convert_fusion.1), channel_id=1, source_target_pairs={{0,8},{1,9},{2,10},{3,11},{4,12},{5,13},{6,14},{7,15},{8,0},{9,1},... | collective-permute-start | bytes 98312 | tf_op jit(solution)/shard_map/ppermute | solution.py:110
  116.9 3.1 %collective-permute-done.12 = bf16[9,2,32,256]{3,2,0,1:T(8,128)(2,1)S(1)} collective-permute-done((bf16[9,2,32,256]{3,2,0,1:T(8,128)(2,1)S(1)}, bf16[9,2,32,256]{3,2,0,1:T(8,128)(2,1)S(1)}, u32[]{:S(2)}, u32[]{:S(2)}) %collective-permute-start.12) | collective-permute-done | bytes 294944 | tf_op jit(solution)/shard_map/ppermute | solution.py:110
  123.4 1.7 %copy.144 = bf16[128,16,256]{2,1,0:T(8,128)(2,1)} copy(bf16[128,16,256]{0,2,1:T(8,128)(2,1)S(1)} %bitcast.339) | data formatting | bytes 2097152
  127.5 2.0 %collective-permute-start.14 = (bf16[9,32,256]{2,1,0:T(8,128)(2,1)S(1)}, bf16[9,32,256]{2,1,0:T(8,128)(2,1)S(1)}, u32[]{:S(2)}, u32[]{:S(2)}) collective-permute-start(bf16[9,32,256]{2,1,0:T(8,128)(2,1)S(1)} %select_convert_fusion), channel_id=1, source_target_pairs={{0,8},{1,9},{2,10},{3,11},{4,12},{5,13},{6,14},{7,15},{8,0},{9,1},... | collective-permute-start | bytes 442376 | tf_op jit(solution)/shard_map/ppermute | solution.py:110
  131.1 4.1 %collective-permute-done.14 = bf16[9,32,256]{2,1,0:T(8,128)(2,1)S(1)} collective-permute-done((bf16[9,32,256]{2,1,0:T(8,128)(2,1)S(1)}, bf16[9,32,256]{2,1,0:T(8,128)(2,1)S(1)}, u32[]{:S(2)}, u32[]{:S(2)}) %collective-permute-start.14) | collective-permute-done | bytes 147488 | tf_op jit(solution)/shard_map/ppermute | solution.py:110
  135.2 1.9 %add_multiply_fusion.1 = f32[9,32,256]{2,1,0:T(8,128)} fusion(bf16[9,32,256]{2,1,0:T(8,128)(2,1)S(1)} %collective-permute-done.14, bf16[9,32,256]{2,1,0:T(8,128)(2,1)S(1)} %collective-permute-done.10, f32[9,2,32,256]{3,2,1,0:T(8,128)} %copy-done.6, s32[]{:T(128)S(6)} %select_n.89, bf16[9,32,256]{2,1,0:T(8,128)(2,1)} %collective-permute-done.13, ...), kind=kLoop, calls=%fused_computation.151 | loop fusion | flops 589824 | bytes 1327113 | tf_op jit(solution)/shard_map/mul | solution.py:226
  (177 shorter events, 52.8 us)
Async XLA Ops:
  0.6 18.4 %copy-start = (bf16[3,3,512,256]{3,2,1,0:T(8,128)(2,1)S(1)}, bf16[3,3,512,256]{3,2,1,0:T(8,128)(2,1)}, u32[]{:S(2)}) copy-start(bf16[3,3,512,256]{3,2,1,0:T(8,128)(2,1)} %param.6) | copy-start | bytes 7077892
  4.2 14.2 %collective-permute-start.1 = (bf16[256,1,128]{2,0,1:T(8,128)(2,1)}, bf16[256,1,128]{2,0,1:T(8,128)(2,1)S(1)}, u32[]{:S(2)}, u32[]{:S(2)}) collective-permute-start(bf16[256,1,128]{2,0,1:T(8,128)(2,1)} %get-tuple-element.36), channel_id=1, source_target_pairs={{0,1},{1,2},{2,3},{3,4},{4,5},{5,6},{6,7},{7,8},{8,9},{9,10},{10,1... | collective-permute-start | bytes 196616 | tf_op jit(solution)/shard_map/ppermute | solution.py:163
  6.6 11.8 %collective-permute-start.2 = (bf16[256,1,128]{2,0,1:T(8,128)(2,1)}, bf16[256,1,128]{2,0,1:T(8,128)(2,1)S(1)}, u32[]{:S(2)}, u32[]{:S(2)}) collective-permute-start(bf16[256,1,128]{2,0,1:T(8,128)(2,1)} %get-tuple-element.37), channel_id=1, source_target_pairs={{1,0},{2,1},{3,2},{4,3},{5,4},{6,5},{7,6},{8,7},{9,8},{10,9},{11,1... | collective-permute-start | bytes 196616 | tf_op jit(solution)/shard_map/ppermute | solution.py:164
  7.9 24.8 %collective-permute-start = (bf16[16,256,128]{2,1,0:T(8,128)(2,1)}, bf16[16,256,128]{2,1,0:T(8,128)(2,1)}, u32[]{:S(2)}, u32[]{:S(2)}) collective-permute-start(bf16[16,256,128]{2,1,0:T(8,128)(2,1)} %bitcast.336), channel_id=1, source_target_pairs={{0,16},{16,0},{1,17},{17,1},{2,18},{18,2},{3,19},{19,3},{4,20},{20... | collective-permute-start | bytes 3145736 | tf_op jit(solution)/shard_map/ppermute | solution.py:110
  10.3 2.9 %copy-start.9 = (bf16[2,2,256,256]{3,2,1,0:T(8,128)(2,1)S(1)}, bf16[2,2,256,256]{3,2,1,0:T(8,128)(2,1)}, u32[]{:S(2)}) copy-start(bf16[2,2,256,256]{3,2,1,0:T(8,128)(2,1)} %param.5) | copy-start | bytes 1572868
  26.7 6.0 %copy-start.3 = (f32[256,8,128]{2,0,1:T(8,128)S(1)}, f32[256,8,128]{2,0,1:T(8,128)}, u32[]{:S(2)}) copy-start(f32[256,8,128]{2,0,1:T(8,128)} %convolution_bitcast_fusion.1) | copy-start | bytes 3145732
  26.7 6.0 %copy-start.8 = (bf16[2,2,128,256]{3,2,1,0:T(8,128)(2,1)S(1)}, bf16[2,2,128,256]{3,2,1,0:T(8,128)(2,1)}, u32[]{:S(2)}) copy-start(bf16[2,2,128,256]{3,2,1,0:T(8,128)(2,1)} %constant_dynamic-slice_fusion.4) | copy-start | bytes 786436
  37.1 33.8 %collective-permute-start.5 = (bf16[256,1,128]{2,0,1:T(8,128)(2,1)}, bf16[256,1,128]{2,0,1:T(8,128)(2,1)}, u32[]{:S(2)}, u32[]{:S(2)}) collective-permute-start(bf16[256,1,128]{2,0,1:T(8,128)(2,1)} %get-tuple-element.34), channel_id=1, source_target_pairs={{0,17},{1,18},{2,19},{3,20},{4,21},{5,22},{6,23},{7,24},{8,25},{9,... | collective-permute-start | bytes 196616 | tf_op jit(solution)/shard_map/ppermute | solution.py:163
  43.0 12.9 %collective-permute-start.3 = (bf16[256,1,128]{2,0,1:T(8,128)(2,1)}, bf16[256,1,128]{2,0,1:T(8,128)(2,1)}, u32[]{:S(2)}, u32[]{:S(2)}) collective-permute-start(bf16[256,1,128]{2,0,1:T(8,128)(2,1)} %get-tuple-element.34), channel_id=1, source_target_pairs={{0,1},{1,2},{2,3},{3,4},{4,5},{5,6},{6,7},{7,8},{8,9},{9,10},{10,1... | collective-permute-start | bytes 196616 | tf_op jit(solution)/shard_map/ppermute | solution.py:163
  48.0 25.9 %collective-permute-start.7 = (bf16[256,1,128]{2,0,1:T(8,128)(2,1)}, bf16[256,1,128]{2,0,1:T(8,128)(2,1)S(1)}, u32[]{:S(2)}, u32[]{:S(2)}) collective-permute-start(bf16[256,1,128]{2,0,1:T(8,128)(2,1)} %get-tuple-element.35), channel_id=1, source_target_pairs={{1,16},{2,17},{3,18},{4,19},{5,20},{6,21},{7,22},{8,23},{9,24},{10... | collective-permute-start | bytes 196616 | tf_op jit(solution)/shard_map/ppermute | solution.py:164
  49.3 10.9 %collective-permute-start.4 = (bf16[256,1,128]{2,0,1:T(8,128)(2,1)}, bf16[256,1,128]{2,0,1:T(8,128)(2,1)}, u32[]{:S(2)}, u32[]{:S(2)}) collective-permute-start(bf16[256,1,128]{2,0,1:T(8,128)(2,1)} %get-tuple-element.35), channel_id=1, source_target_pairs={{1,0},{2,1},{3,2},{4,3},{5,4},{6,5},{7,6},{8,7},{9,8},{10,9},{11,1... | collective-permute-start | bytes 196616 | tf_op jit(solution)/shard_map/ppermute | solution.py:164
  52.7 19.8 %collective-permute-start.6 = (bf16[256,8,128]{2,0,1:T(8,128)(2,1)}, bf16[256,8,128]{2,0,1:T(8,128)(2,1)}, u32[]{:S(2)}, u32[]{:S(2)}) collective-permute-start(bf16[256,8,128]{2,0,1:T(8,128)(2,1)} %get-tuple-element.15), channel_id=1, source_target_pairs={{0,16},{16,0},{1,17},{17,1},{2,18},{18,2},{3,19},{19,3},{4,20},{20... | collective-permute-start | bytes 1572872 | tf_op jit(solution)/shard_map/ppermute | solution.py:110
  55.9 24.8 %collective-permute-start.15 = (bf16[256,8,128]{2,0,1:T(8,128)(2,1)}, bf16[256,8,128]{2,0,1:T(8,128)(2,1)S(1)}, u32[]{:S(2)}, u32[]{:S(2)}) collective-permute-start(bf16[256,8,128]{2,0,1:T(8,128)(2,1)} %fusion.16), channel_id=1, source_target_pairs={{0,16},{16,0},{1,17},{17,1},{2,18},{18,2},{3,19},{19,3},{4,20},{20... | collective-permute-start | bytes 1572872 | tf_op jit(solution)/shard_map/ppermute | solution.py:110
  69.5 25.2 %collective-permute-start.8 = (bf16[9,2,2,32,256]{4,3,2,1,0:T(8,128)(2,1)S(1)}, bf16[9,2,2,32,256]{4,3,2,1,0:T(8,128)(2,1)S(1)}, u32[]{:S(2)}, u32[]{:S(2)}) collective-permute-start(bf16[9,2,2,32,256]{4,3,2,1,0:T(8,128)(2,1)S(1)} %fusion.28), channel_id=1, source_target_pairs={{0,1},{1,0},{2,3},{3,2},{4,5},{5,4},{6,7},{7,6},{8,9},{9,8},{10,11... | collective-permute-start | bytes 1769480 | tf_op jit(solution)/shard_map/ppermute | solution.py:110
  82.1 31.7 %collective-permute-start.22 = (bf16[256,8,128]{2,0,1:T(8,128)(2,1)S(1)}, bf16[256,8,128]{2,0,1:T(8,128)(2,1)S(1)}, u32[]{:S(2)}, u32[]{:S(2)}) collective-permute-start(bf16[256,8,128]{2,0,1:T(8,128)(2,1)S(1)} %fusion.17), channel_id=1, source_target_pairs={{0,16},{16,0},{1,17},{17,1},{2,18},{18,2},{3,19},{19,3},{4,20},{20... | collective-permute-start | bytes 1572872 | tf_op jit(solution)/shard_map/ppermute | solution.py:110
  85.2 6.5 %collective-permute-start.19 = (bf16[4,2,2,16,256]{4,3,0,2,1:T(8,128)(2,1)S(1)}, bf16[4,2,2,16,256]{4,3,0,2,1:T(8,128)(2,1)S(1)}, u32[]{:S(2)}, u32[]{:S(2)}) collective-permute-start(bf16[4,2,2,16,256]{4,3,0,2,1:T(8,128)(2,1)S(1)} %fusion.107), channel_id=1, source_target_pairs={{0,1},{1,0},{2,3},{3,2},{4,5},{5,4},{6,7},{7,6},{8,9},{9,8},{10,11... | collective-permute-start | bytes 393224 | tf_op jit(solution)/shard_map/ppermute | solution.py:110
  85.5 6.4 %collective-permute-start.16 = (bf16[4,2,2,16,256]{4,3,2,1,0:T(8,128)(2,1)S(1)}, bf16[4,2,2,16,256]{4,3,2,1,0:T(8,128)(2,1)S(1)}, u32[]{:S(2)}, u32[]{:S(2)}) collective-permute-start(bf16[4,2,2,16,256]{4,3,2,1,0:T(8,128)(2,1)S(1)} %fusion.106), channel_id=1, source_target_pairs={{0,1},{1,0},{2,3},{3,2},{4,5},{5,4},{6,7},{7,6},{8,9},{9,8},{10,11... | collective-permute-start | bytes 393224 | tf_op jit(solution)/shard_map/ppermute | solution.py:110
  86.0 35.8 %collective-permute-start.24 = (bf16[2,2,128,256]{2,3,1,0:T(8,128)(2,1)S(1)}, bf16[2,2,128,256]{2,3,1,0:T(8,128)(2,1)S(1)}, u32[]{:S(2)}, u32[]{:S(2)}) collective-permute-start(bf16[2,2,128,256]{2,3,1,0:T(8,128)(2,1)S(1)} %copy-done.16), channel_id=1, source_target_pairs={{0,16},{16,0},{1,17},{17,1},{2,18},{18,2},{3,19},{19,3},{4,20},{20... | collective-permute-start | bytes 786440 | tf_op jit(solution)/shard_map/ppermute | solution.py:110
  91.7 19.0 %collective-permute-start.11 = (bf16[9,2,2,32,256]{4,3,0,2,1:T(8,128)(2,1)S(1)}, bf16[9,2,2,32,256]{4,3,0,2,1:T(8,128)(2,1)S(1)}, u32[]{:S(2)}, u32[]{:S(2)}) collective-permute-start(bf16[9,2,2,32,256]{4,3,0,2,1:T(8,128)(2,1)S(1)} %fusion.29), channel_id=1, source_target_pairs={{0,1},{1,0},{2,3},{3,2},{4,5},{5,4},{6,7},{7,6},{8,9},{9,8},{10,11... | collective-permute-start | bytes 1769480 | tf_op jit(solution)/shard_map/ppermute | solution.py:110
  91.9 5.4 %collective-permute-start.20 = (bf16[4,2,16,256]{3,2,0,1:T(8,128)(2,1)S(1)}, bf16[4,2,16,256]{3,2,0,1:T(8,128)(2,1)S(1)}, u32[]{:S(2)}, u32[]{:S(2)}) collective-permute-start(bf16[4,2,16,256]{3,2,0,1:T(8,128)(2,1)S(1)} %fusion.109), channel_id=1, source_target_pairs={{0,4},{1,5},{2,6},{3,7},{4,0},{5,1},{6,2},{7,3},{8,12},{9,13},{10,... | collective-permute-start | bytes 196616 | tf_op jit(solution)/shard_map/ppermute | solution.py:110
  94.8 4.3 %collective-permute-start.17 = (bf16[4,2,16,256]{3,2,1,0:T(8,128)(2,1)S(1)}, bf16[4,2,16,256]{3,2,1,0:T(8,128)(2,1)S(1)}, u32[]{:S(2)}, u32[]{:S(2)}) collective-permute-start(bf16[4,2,16,256]{3,2,1,0:T(8,128)(2,1)S(1)} %fusion.108), channel_id=1, source_target_pairs={{0,2},{1,3},{2,0},{3,1},{4,6},{5,7},{6,4},{7,5},{8,10},{9,11},{10,... | collective-permute-start | bytes 196616 | tf_op jit(solution)/shard_map/ppermute | solution.py:110
  97.3 13.3 %collective-permute-start.9 = (bf16[9,2,32,256]{3,2,1,0:T(8,128)(2,1)S(1)}, bf16[9,2,32,256]{3,2,1,0:T(8,128)(2,1)S(1)}, u32[]{:S(2)}, u32[]{:S(2)}) collective-permute-start(bf16[9,2,32,256]{3,2,1,0:T(8,128)(2,1)S(1)} %fusion.96), channel_id=1, source_target_pairs={{0,2},{1,3},{2,0},{3,1},{4,6},{5,7},{6,4},{7,5},{8,10},{9,11},{10,... | collective-permute-start | bytes 884744 | tf_op jit(solution)/shard_map/ppermute | solution.py:110
  99.1 7.6 %collective-permute-start.21 = (bf16[4,16,256]{2,1,0:T(8,128)(2,1)S(1)}, bf16[4,16,256]{2,1,0:T(8,128)(2,1)S(1)}, u32[]{:S(2)}, u32[]{:S(2)}) collective-permute-start(bf16[4,16,256]{2,1,0:T(8,128)(2,1)S(1)} %fusion.111), channel_id=1, source_target_pairs={{0,2},{1,3},{2,0},{3,1},{4,6},{5,7},{6,4},{7,5},{8,10},{9,11},{10,... | collective-permute-start | bytes 98312 | tf_op jit(solution)/shard_map/ppermute | solution.py:110
  106.7 3.9 %collective-permute-start.18 = (bf16[4,16,256]{2,1,0:T(8,128)(2,1)S(1)}, bf16[4,16,256]{2,1,0:T(8,128)(2,1)S(1)}, u32[]{:S(2)}, u32[]{:S(2)}) collective-permute-start(bf16[4,16,256]{2,1,0:T(8,128)(2,1)S(1)} %fusion.110), channel_id=1, source_target_pairs={{0,4},{1,5},{2,6},{3,7},{4,0},{5,1},{6,2},{7,3},{8,12},{9,13},{10,... | collective-permute-start | bytes 98312 | tf_op jit(solution)/shard_map/ppermute | solution.py:110
  108.2 5.5 %copy-start.14 = (f32[4,16,256]{2,1,0:T(8,128)}, f32[4,16,256]{2,1,0:T(8,128)S(1)}, u32[]{:S(2)}) copy-start(f32[4,16,256]{2,1,0:T(8,128)S(1)} %bitcast_add_fusion.9) | copy-start | bytes 196612
  110.6 3.1 %copy-start.15 = (f32[4,16,256]{2,1,0:T(8,128)}, f32[4,16,256]{2,1,0:T(8,128)S(1)}, u32[]{:S(2)}) copy-start(f32[4,16,256]{2,1,0:T(8,128)S(1)} %bitcast_add_fusion.10) | copy-start | bytes 196612
  110.7 9.3 %copy-start.6 = (f32[9,2,32,256]{3,2,1,0:T(8,128)}, f32[9,2,32,256]{3,2,1,0:T(8,128)S(1)}, u32[]{:S(2)}) copy-start(f32[9,2,32,256]{3,2,1,0:T(8,128)S(1)} %bitcast_add_fusion.2) | copy-start | bytes 1769476
  111.0 9.0 %collective-permute-start.12 = (bf16[9,2,32,256]{3,2,0,1:T(8,128)(2,1)S(1)}, bf16[9,2,32,256]{3,2,0,1:T(8,128)(2,1)S(1)}, u32[]{:S(2)}, u32[]{:S(2)}) collective-permute-start(bf16[9,2,32,256]{3,2,0,1:T(8,128)(2,1)S(1)} %fusion.97), channel_id=1, source_target_pairs={{0,4},{1,5},{2,6},{3,7},{4,0},{5,1},{6,2},{7,3},{8,12},{9,13},{10,... | collective-permute-start | bytes 884744 | tf_op jit(solution)/shard_map/ppermute | solution.py:110
  113.3 11.8 %collective-permute-start.10 = (bf16[9,32,256]{2,1,0:T(8,128)(2,1)}, bf16[9,32,256]{2,1,0:T(8,128)(2,1)S(1)}, u32[]{:S(2)}, u32[]{:S(2)}) collective-permute-start(bf16[9,32,256]{2,1,0:T(8,128)(2,1)} %fusion.104), channel_id=1, source_target_pairs={{0,4},{1,5},{2,6},{3,7},{4,0},{5,1},{6,2},{7,3},{8,12},{9,13},{10,... | collective-permute-start | bytes 442376 | tf_op jit(solution)/shard_map/ppermute | solution.py:110
  114.4 15.1 %collective-permute-start.23 = (bf16[4,16,256]{2,1,0:T(8,128)(2,1)}, bf16[4,16,256]{2,1,0:T(8,128)(2,1)}, u32[]{:S(2)}, u32[]{:S(2)}) collective-permute-start(bf16[4,16,256]{2,1,0:T(8,128)(2,1)} %select_convert_fusion.1), channel_id=1, source_target_pairs={{0,8},{1,9},{2,10},{3,11},{4,12},{5,13},{6,14},{7,15},{8,0},{9,1},... | collective-permute-start | bytes 98312 | tf_op jit(solution)/shard_map/ppermute | solution.py:110
  120.9 5.5 %collective-permute-start.13 = (bf16[9,32,256]{2,1,0:T(8,128)(2,1)}, bf16[9,32,256]{2,1,0:T(8,128)(2,1)}, u32[]{:S(2)}, u32[]{:S(2)}) collective-permute-start(bf16[9,32,256]{2,1,0:T(8,128)(2,1)} %fusion.105), channel_id=1, source_target_pairs={{0,2},{1,3},{2,0},{3,1},{4,6},{5,7},{6,4},{7,5},{8,10},{9,11},{10,... | collective-permute-start | bytes 442376 | tf_op jit(solution)/shard_map/ppermute | solution.py:110
  127.5 7.7 %collective-permute-start.14 = (bf16[9,32,256]{2,1,0:T(8,128)(2,1)S(1)}, bf16[9,32,256]{2,1,0:T(8,128)(2,1)S(1)}, u32[]{:S(2)}, u32[]{:S(2)}) collective-permute-start(bf16[9,32,256]{2,1,0:T(8,128)(2,1)S(1)} %select_convert_fusion), channel_id=1, source_target_pairs={{0,8},{1,9},{2,10},{3,11},{4,12},{5,13},{6,14},{7,15},{8,0},{9,1},... | collective-permute-start | bytes 442376 | tf_op jit(solution)/shard_map/ppermute | solution.py:110
  (10 other events, 19.0 us)

commit v4 on v2

--- a/solution.py
+++ b/solution.py
@@ -136,14 +136,18 @@
     own_bits = list(range(top))
     other_bits = own_bits[:1] + own_bits[:0:-1]
     sums = []
-    for block, order in ((own, own_bits), (other, other_bits)):
+    parts = ((own, own_bits), (other, other_bits))
+    if swapped is not None:
+        parts = ((jnp.concatenate([own, other]), own_bits),)
+    for block, order in parts:
         left = list(range(top))[::-1]
-        block = block.reshape((taps,) + (2,) * top + (share, depth))
+        block = block.reshape((block.shape[0],) + (2,) * top + (share, depth))
         for bit in order:
             block = halve(block, 1 + left.index(bit), bit)
             left.remove(bit)
         sums.append(block)
     if swapped is not None:
+        sums = [sums[0][:taps], sums[0][taps:]]
         sums, swapped = lax.optimization_barrier((sums, swapped))
     here = (lax.axis_index("tile") >> top) == lax.axis_index("chan")
     keep = jnp.where(here, sums[0], sums[1])

time: 133 us -> 125 us (0.940)
  starting transfers between devices: 38.5 us -> 33.3 us
  waiting for transfers between devices: 32.5 us -> 28.1 us
  local copies, waits for them, and re-layouts: 18.6 us -> 20.8 us
    ppermute x19 -> x16, starting transfers between devices: 27.1 us -> 21.9 us  [flip(): return lax.ppermute(block, axis, [(i, i ^ mask) for i in range(count)])]
    ppermute x19 -> x16, waiting for transfers between devices: 32.3 us -> 28.1 us  [flip(): return lax.ppermute(block, axis, [(i, i ^ mask) for i in range(count)])]
    dot_general x2, local copies, waits for them, and re-layouts: 5.36 us -> 7.36 us  [down_terms(): jnp.einsum('rawbc,drw->abcd', patches, grad_pre, preferred_element_type=f32)]
    unnamed x66 -> x65, local copies, waits for them, and re-layouts: 9.34 us -> 8.88 us
  transfers between devices with their start and end apart: 25 -> 22, of which waited for: 10 -> 7; matrix products, arithmetic and copies ran while one was open for 38% -> 42% of each run, Pallas kernels for 0% -> 0%
where the time goes in v4:
time: 125 us
  matrix products  33.5 us (27%)
  starting transfers between devices  33.3 us (27%)
  waiting for transfers between devices  28.1 us (22%)
  local copies, waits for them, and re-layouts  20.8 us (17%)
  other arithmetic  7.2 us (6%)
  between operations  1.73 us (1%)
    ppermute x16, waiting for transfers between devices, flip(): return lax.ppermute(block, axis, [(i, i ^ mask) for i in range(count)])  28.1 us
    ppermute x16, starting transfers between devices, flip(): return lax.ppermute(block, axis, [(i, i ^ mask) for i in range(count)])  21.9 us
    dot_general x36, matrix products, tap_sum(): jnp.einsum(form, window, weights[i, j], preferred_element_type=jnp.float32)  19 us
    unnamed x65, local copies, waits for them, and re-layouts  8.88 us
    dot_general x18, matrix products, mix_terms(): jnp.einsum('crw,drw->cd', window, cotangent, preferred_element_type=f32)  8.19 us
    ppermute x3, starting transfers between devices, edge_rows(): low = lax.ppermute(block[:, -1:], ('chan', 'tile'), down)  7.53 us
    dot_general x2, local copies, waits for them, and re-layouts, down_terms(): jnp.einsum('rawbc,drw->abcd', patches, grad_pre, preferred_element_type=f32)  7.36 us
    ppermute x3, starting transfers between devices, edge_rows(): high = lax.ppermute(block[:, :1], ('chan', 'tile'), up)  3.86 us
  transfers between devices with their start and end apart: 22, of which 7 were waited for; matrix products, arithmetic and copies ran while one was open for 42% of the time, Pallas kernels for 0%

profile of v4, /device:TPU:0, one launch (start us, length us, event | category | flops | bytes accessed | tf_op | source)
XLA Modules:
  0.0 124.6 jit_solution(16886615076769808564)
XLA Ops:
  0.7 2.8 %copy.240 = bf16[128,16,256]{0,2,1:T(8,128)(2,1)} copy(bf16[128,16,256]{2,1,0:T(8,128)(2,1)} %param.4) | data formatting | bytes 2097152 | tf_op args[0]
  4.3 1.3 %collective-permute-start.6 = (bf16[256,1,128]{2,0,1:T(8,128)(2,1)}, bf16[256,1,128]{2,0,1:T(8,128)(2,1)S(1)}, u32[]{:S(2)}, u32[]{:S(2)}) collective-permute-start(bf16[256,1,128]{2,0,1:T(8,128)(2,1)} %get-tuple-element.35), channel_id=1, source_target_pairs={{1,0},{2,1},{3,2},{4,3},{5,4},{6,5},{7,6},{8,7},{9,8},{10,9},{11,1... | collective-permute-start | bytes 196616 | tf_op jit(solution)/shard_map/ppermute | solution.py:168
  5.6 3.0 %collective-permute-start.5 = (bf16[256,1,128]{2,0,1:T(8,128)(2,1)}, bf16[256,1,128]{2,0,1:T(8,128)(2,1)S(1)}, u32[]{:S(2)}, u32[]{:S(2)}) collective-permute-start(bf16[256,1,128]{2,0,1:T(8,128)(2,1)} %get-tuple-element.34), channel_id=1, source_target_pairs={{0,1},{1,2},{2,3},{3,4},{4,5},{5,6},{6,7},{7,8},{8,9},{9,10},{10,1... | collective-permute-start | bytes 196616 | tf_op jit(solution)/shard_map/ppermute | solution.py:167
  8.6 3.0 %collective-permute-start = (bf16[16,256,128]{2,1,0:T(8,128)(2,1)}, bf16[16,256,128]{2,1,0:T(8,128)(2,1)}, u32[]{:S(2)}, u32[]{:S(2)}) collective-permute-start(bf16[16,256,128]{2,1,0:T(8,128)(2,1)} %bitcast.325), channel_id=1, source_target_pairs={{0,16},{16,0},{1,17},{17,1},{2,18},{18,2},{3,19},{19,3},{4,20},{20... | collective-permute-start | bytes 3145736 | tf_op jit(solution)/shard_map/ppermute | solution.py:110
  11.7 3.7 %copy.452 = bf16[2,2,128,8,128]{4,2,3,1,0:T(8,128)(2,1)} copy(bf16[2,2,128,8,128]{2,1,4,0,3:T(2,128)(2,1)} %bitcast.326) | data formatting | bytes 2097152 | tf_op jit(solution)/shard_map/rawbc,drw->abcd/dot_general | solution.py:235
  15.4 1.8 %convolution_bitcast_fusion.1 = f32[256,8,128]{0,2,1:T(8,128)S(1)} fusion(bf16[8,2,128,2,128]{4,3,2,1,0:T(2,128)(2,1)} %bitcast.327, bf16[2,2,256,256]{3,2,1,0:T(8,128)(2,1)} %param.5, s32[]{:T(128)S(6)} %select_n.74), kind=kOutput, calls=%fused_computation.48 | convolution fusion | flops 268435456 | bytes 2359300 | tf_op jit(solution)/shard_map/rawbc,abcd->drw/dot_general | solution.py:203
  20.7 1.6 %convolution_add_fusion.1 = f32[256,8,128]{0,2,1:T(8,128)} fusion(f32[256,8,128]{0,2,1:T(8,128)S(1)} %convolution_add_fusion.2, bf16[256,10,130]{2,0,1:T(8,128)(2,1)S(1)} %fusion.15, bf16[3,3,512,256]{3,2,1,0:T(8,128)(2,1)S(1)} %copy-done, s32[]{:T(128)S(6)} %add.270, s32[]{:T(128)S(6)} %select_n.73), kind=kOutput, calls=%fused_computation.16 | convolution fusion | flops 134479872 | bytes 2752520 | tf_op jit(solution)/shard_map/drw,cd->crw/dot_general | solution.py:120
  25.0 1.4 %fusion.73 = f32[256,8,128]{0,2,1:T(8,128)} fusion(bf16[256,10,130]{2,0,1:T(8,128)(2,1)S(1)} %fusion.15, bf16[3,3,512,256]{3,2,1,0:T(8,128)(2,1)S(1)} %copy-done, s32[]{:T(128)S(6)} %add.270, s32[]{:T(128)S(6)} %select_n.73), kind=kOutput, calls=%fused_computation.129 | convolution fusion | flops 134217728 | bytes 1703944 | tf_op jit(solution)/shard_map/drw,cd->crw/dot_general | solution.py:120
  27.4 1.2 fusion.17
  28.6 6.8 %collective-permute-done = bf16[16,256,128]{2,1,0:T(8,128)(2,1)} collective-permute-done((bf16[16,256,128]{2,1,0:T(8,128)(2,1)}, bf16[16,256,128]{2,1,0:T(8,128)(2,1)}, u32[]{:S(2)}, u32[]{:S(2)}) %collective-permute-start) | collective-permute-done | bytes 1048608 | tf_op jit(solution)/shard_map/ppermute | solution.py:110
  35.4 2.7 %multiply_convert_fusion = (bf16[256,8,128]{0,2,1:T(8,128)(2,1)S(1)}, f32[256,8,128]{0,2,1:T(8,128)}) fusion(f32[256,8,128]{0,2,1:T(8,128)S(1)} %convolution_bitcast_fusion.1, bf16[8,2,128,2,128]{4,3,2,1,0:T(2,128)(2,1)} %bitcast.10, bf16[2,2,128,256]{3,2,1,0:T(8,128)(2,1)S(1)} %constant_dynamic-slice_fusion.2), kind=kOutput, calls=%fused_computation.69 | convolution fusion | flops 270008320 | bytes 3932160 | tf_op jit(solution)/shard_map/rawbc,abcd->drw/dot_general | solution.py:204
  38.1 2.5 %collective-permute-start.4 = (bf16[256,8,128]{0,2,1:T(8,128)(2,1)S(1)}, bf16[256,8,128]{0,2,1:T(8,128)(2,1)}, u32[]{:S(2)}, u32[]{:S(2)}) collective-permute-start(bf16[256,8,128]{0,2,1:T(8,128)(2,1)S(1)} %get-tuple-element.40), channel_id=1, source_target_pairs={{0,16},{16,0},{1,17},{17,1},{2,18},{18,2},{3,19},{19,3},{4,20},{20... | collective-permute-start | bytes 1572872 | tf_op jit(solution)/shard_map/ppermute | solution.py:110
  41.2 2.2 %collective-permute-start.3 = (bf16[256,1,128]{0,2,1:T(8,128)(2,1)}, bf16[256,1,128]{0,2,1:T(8,128)(2,1)}, u32[]{:S(2)}, u32[]{:S(2)}) collective-permute-start(bf16[256,1,128]{0,2,1:T(8,128)(2,1)} %get-tuple-element.36), channel_id=1, source_target_pairs={{0,17},{1,18},{2,19},{3,20},{4,21},{5,22},{6,23},{7,24},{8,25},{9,... | collective-permute-start | bytes 196616 | tf_op jit(solution)/shard_map/ppermute | solution.py:167
  43.4 2.3 %collective-permute-start.1 = (bf16[256,1,128]{0,2,1:T(8,128)(2,1)}, bf16[256,1,128]{0,2,1:T(8,128)(2,1)S(1)}, u32[]{:S(2)}, u32[]{:S(2)}) collective-permute-start(bf16[256,1,128]{0,2,1:T(8,128)(2,1)} %get-tuple-element.36), channel_id=1, source_target_pairs={{0,1},{1,2},{2,3},{3,4},{4,5},{5,6},{6,7},{7,8},{8,9},{9,10},{10,1... | collective-permute-start | bytes 196616 | tf_op jit(solution)/shard_map/ppermute | solution.py:167
  45.7 1.3 %collective-permute-start.7 = (bf16[256,1,128]{0,2,1:T(8,128)(2,1)}, bf16[256,1,128]{0,2,1:T(8,128)(2,1)}, u32[]{:S(2)}, u32[]{:S(2)}) collective-permute-start(bf16[256,1,128]{0,2,1:T(8,128)(2,1)} %get-tuple-element.37), channel_id=1, source_target_pairs={{1,16},{2,17},{3,18},{4,19},{5,20},{6,21},{7,22},{8,23},{9,24},{10... | collective-permute-start | bytes 196616 | tf_op jit(solution)/shard_map/ppermute | solution.py:168
  47.0 1.3 %collective-permute-start.2 = (bf16[256,1,128]{0,2,1:T(8,128)(2,1)}, bf16[256,1,128]{0,2,1:T(8,128)(2,1)S(1)}, u32[]{:S(2)}, u32[]{:S(2)}) collective-permute-start(bf16[256,1,128]{0,2,1:T(8,128)(2,1)} %get-tuple-element.37), channel_id=1, source_target_pairs={{1,0},{2,1},{3,2},{4,3},{5,4},{6,5},{7,6},{8,7},{9,8},{10,9},{11,1... | collective-permute-start | bytes 196616 | tf_op jit(solution)/shard_map/ppermute | solution.py:168
  49.4 3.6 %copy.352 = bf16[2,2,128,8,128]{4,2,3,1,0:T(8,128)(2,1)} copy(bf16[2,2,128,8,128]{2,1,4,0,3:T(2,128)(2,1)} %bitcast.130) | data formatting | bytes 2097152 | tf_op jit(solution)/shard_map/rawbc,drw->abcd/dot_general | solution.py:235
  57.0 3.0 %collective-permute-start.8 = (bf16[9,2,2,32,256]{4,3,2,1,0:T(8,128)(2,1)S(1)}, bf16[9,2,2,32,256]{4,3,2,1,0:T(8,128)(2,1)S(1)}, u32[]{:S(2)}, u32[]{:S(2)}) collective-permute-start(bf16[9,2,2,32,256]{4,3,2,1,0:T(8,128)(2,1)S(1)} %fusion.28), channel_id=1, source_target_pairs={{0,1},{1,0},{2,3},{3,2},{4,5},{5,4},{6,7},{7,6},{8,9},{9,8},{10,11... | collective-permute-start | bytes 1769480 | tf_op jit(solution)/shard_map/ppermute | solution.py:110
  64.1 1.3 %select_maximum_fusion = bf16[256,10,130]{0,2,1:T(8,128)(2,1)S(1)} fusion(bf16[256,1,128]{0,2,1:T(8,128)(2,1)} %collective-permute-done.7, bf16[256,8,128]{0,2,1:T(8,128)(2,1)} %collective-permute-done.4, bf16[256,1,128]{0,2,1:T(8,128)(2,1)} %collective-permute-done.3), kind=kLoop, calls=%fused_computation.71 | loop fusion | flops 3993600 | bytes 1320960 | tf_op jit(solution)/shard_map/concatenate | solution.py:174
  66.4 1.4 %fusion.173 = f32[256,256,1]{1,0,2:T(8,128)S(1)} fusion(bf16[256,8,128]{0,2,1:T(8,128)(2,1)} %collective-permute-done.4, bf16[256,8,128]{2,1,0:T(8,128)(2,1)S(1)} %copy-done.1), kind=kOutput, calls=%fused_computation.284 | convolution fusion | flops 134217728 | bytes 1310720 | tf_op jit(solution)/shard_map/crw,drw->cd/dot_general | solution.py:223
  72.2 1.4 %collective-permute-start.21 = (bf16[2,2,128,256]{3,2,1,0:T(8,128)(2,1)S(1)}, bf16[2,2,128,256]{3,2,1,0:T(8,128)(2,1)S(1)}, u32[]{:S(2)}, u32[]{:S(2)}) collective-permute-start(bf16[2,2,128,256]{3,2,1,0:T(8,128)(2,1)S(1)} %copy-done.15), channel_id=1, source_target_pairs={{0,16},{16,0},{1,17},{17,1},{2,18},{18,2},{3,19},{19,3},{4,20},{20... | collective-permute-start | bytes 786440 | tf_op jit(solution)/shard_map/ppermute | solution.py:110
  76.3 1.4 %fusion.11 = f32[256,8,128]{2,0,1:T(8,128)S(1)} fusion(f32[256,8,128]{2,0,1:T(8,128)S(1)} %fusion.62, f32[256,8,128]{2,0,1:T(8,128)S(1)} %convolution_add_fusion.10, bf16[256,8,128]{0,2,1:T(8,128)(2,1)} %collective-permute-done.4, bf16[3,3,512,256]{3,2,1,0:T(8,128)(2,1)S(1)} %copy-done, s32[]{:T(128)S(6)} %add.269, s32[]{:T(128)S(6)} %select_n.76), kind=kOutput, calls=%fused_computation.27 | convolution fusion | flops 134742016 | bytes 3801096 | tf_op jit(solution)/shard_map/crw,cd->drw/dot_general | solution.py:120
  78.4 2.8 %collective-permute-start.9 = (bf16[9,2,32,256]{3,2,1,0:T(8,128)(2,1)S(1)}, bf16[9,2,32,256]{3,2,1,0:T(8,128)(2,1)S(1)}, u32[]{:S(2)}, u32[]{:S(2)}) collective-permute-start(bf16[9,2,32,256]{3,2,1,0:T(8,128)(2,1)S(1)} %fusion.108), channel_id=1, source_target_pairs={{0,2},{1,3},{2,0},{3,1},{4,6},{5,7},{6,4},{7,5},{8,10},{9,11},{10,... | collective-permute-start | bytes 884744 | tf_op jit(solution)/shard_map/ppermute | solution.py:110
  83.1 5.8 %collective-permute-done.9 = bf16[9,2,32,256]{3,2,1,0:T(8,128)(2,1)S(1)} collective-permute-done((bf16[9,2,32,256]{3,2,1,0:T(8,128)(2,1)S(1)}, bf16[9,2,32,256]{3,2,1,0:T(8,128)(2,1)S(1)}, u32[]{:S(2)}, u32[]{:S(2)}) %collective-permute-start.9) | collective-permute-done | bytes 294944 | tf_op jit(solution)/shard_map/ppermute | solution.py:110
  89.0 2.8 %collective-permute-start.10 = (bf16[9,32,256]{2,1,0:T(8,128)(2,1)S(1)}, bf16[9,32,256]{2,1,0:T(8,128)(2,1)S(1)}, u32[]{:S(2)}, u32[]{:S(2)}) collective-permute-start(bf16[9,32,256]{2,1,0:T(8,128)(2,1)S(1)} %fusion.117), channel_id=1, source_target_pairs={{0,4},{1,5},{2,6},{3,7},{4,0},{5,1},{6,2},{7,3},{8,12},{9,13},{10,... | collective-permute-start | bytes 442376 | tf_op jit(solution)/shard_map/ppermute | solution.py:110
  96.8 7.8 %collective-permute-done.12 = bf16[9,2,32,256]{3,2,0,1:T(8,128)(2,1)S(1)} collective-permute-done((bf16[9,2,32,256]{3,2,0,1:T(8,128)(2,1)S(1)}, bf16[9,2,32,256]{3,2,0,1:T(8,128)(2,1)S(1)}, u32[]{:S(2)}, u32[]{:S(2)}) %collective-permute-start.12) | collective-permute-done | bytes 294944 | tf_op jit(solution)/shard_map/ppermute | solution.py:110
  106.0 3.1 %collective-permute-done.18 = bf16[8,16,256]{2,1,0:T(8,128)(2,1)S(1)} collective-permute-done((bf16[8,16,256]{2,1,0:T(8,128)(2,1)S(1)}, bf16[8,16,256]{2,1,0:T(8,128)(2,1)S(1)}, u32[]{:S(2)}, u32[]{:S(2)}) %collective-permute-start.18) | collective-permute-done | bytes 65568 | tf_op jit(solution)/shard_map/ppermute | solution.py:110
  109.2 1.2 collective-permute-done.13
  111.1 2.8 %collective-permute-start.14 = (bf16[9,32,256]{2,1,0:T(8,128)(2,1)}, bf16[9,32,256]{2,1,0:T(8,128)(2,1)}, u32[]{:S(2)}, u32[]{:S(2)}) collective-permute-start(bf16[9,32,256]{2,1,0:T(8,128)(2,1)} %select_convert_fusion), channel_id=1, source_target_pairs={{0,8},{1,9},{2,10},{3,11},{4,12},{5,13},{6,14},{7,15},{8,0},{9,1},... | collective-permute-start | bytes 442376 | tf_op jit(solution)/shard_map/ppermute | solution.py:110
  116.3 1.7 %copy.357 = bf16[128,16,256]{2,1,0:T(8,128)(2,1)} copy(bf16[128,16,256]{0,2,1:T(8,128)(2,1)S(1)} %bitcast.330) | data formatting | bytes 2097152
  118.0 3.1 %collective-permute-done.20 = bf16[4,16,256]{2,1,0:T(8,128)(2,1)} collective-permute-done((bf16[4,16,256]{2,1,0:T(8,128)(2,1)}, bf16[4,16,256]{2,1,0:T(8,128)(2,1)}, u32[]{:S(2)}, u32[]{:S(2)}) %collective-permute-start.20) | collective-permute-done | bytes 32800 | tf_op jit(solution)/shard_map/ppermute | solution.py:110
  122.6 2.0 %add_multiply_fusion.1 = f32[9,32,256]{2,1,0:T(8,128)} fusion(bf16[9,32,256]{2,1,0:T(8,128)(2,1)} %collective-permute-done.14, bf16[9,32,256]{2,1,0:T(8,128)(2,1)S(1)} %collective-permute-done.10, f32[9,2,32,256]{3,2,1,0:T(8,128)} %copy-done.9, s32[]{:T(128)S(6)} %select_n.82, bf16[9,32,256]{2,1,0:T(8,128)(2,1)} %copy-done.16, ...), kind=kLoop, calls=%fused_computation.168 | loop fusion | flops 589824 | bytes 1327113 | tf_op jit(solution)/shard_map/mul | solution.py:229
  (173 shorter events, 38.8 us)
Async XLA Ops:
  0.6 17.3 %copy-start = (bf16[3,3,512,256]{3,2,1,0:T(8,128)(2,1)S(1)}, bf16[3,3,512,256]{3,2,1,0:T(8,128)(2,1)}, u32[]{:S(2)}) copy-start(bf16[3,3,512,256]{3,2,1,0:T(8,128)(2,1)} %param.6) | copy-start | bytes 7077892
  3.6 23.8 %copy-start.2 = (bf16[256,8,128]{2,0,1:T(8,128)(2,1)}, bf16[256,8,128]{2,0,1:T(8,128)(2,1)S(1)}, u32[]{:S(2)}) copy-start(bf16[256,8,128]{2,0,1:T(8,128)(2,1)S(1)} %copy.252) | copy-start | bytes 1572868
  4.3 12.9 %collective-permute-start.6 = (bf16[256,1,128]{2,0,1:T(8,128)(2,1)}, bf16[256,1,128]{2,0,1:T(8,128)(2,1)S(1)}, u32[]{:S(2)}, u32[]{:S(2)}) collective-permute-start(bf16[256,1,128]{2,0,1:T(8,128)(2,1)} %get-tuple-element.35), channel_id=1, source_target_pairs={{1,0},{2,1},{3,2},{4,3},{5,4},{6,5},{7,6},{8,7},{9,8},{10,9},{11,1... | collective-permute-start | bytes 196616 | tf_op jit(solution)/shard_map/ppermute | solution.py:168
  5.6 11.7 %collective-permute-start.5 = (bf16[256,1,128]{2,0,1:T(8,128)(2,1)}, bf16[256,1,128]{2,0,1:T(8,128)(2,1)S(1)}, u32[]{:S(2)}, u32[]{:S(2)}) collective-permute-start(bf16[256,1,128]{2,0,1:T(8,128)(2,1)} %get-tuple-element.34), channel_id=1, source_target_pairs={{0,1},{1,2},{2,3},{3,4},{4,5},{5,6},{6,7},{7,8},{8,9},{9,10},{10,1... | collective-permute-start | bytes 196616 | tf_op jit(solution)/shard_map/ppermute | solution.py:167
  8.6 26.8 %collective-permute-start = (bf16[16,256,128]{2,1,0:T(8,128)(2,1)}, bf16[16,256,128]{2,1,0:T(8,128)(2,1)}, u32[]{:S(2)}, u32[]{:S(2)}) collective-permute-start(bf16[16,256,128]{2,1,0:T(8,128)(2,1)} %bitcast.325), channel_id=1, source_target_pairs={{0,16},{16,0},{1,17},{17,1},{2,18},{18,2},{3,19},{19,3},{4,20},{20... | collective-permute-start | bytes 3145736 | tf_op jit(solution)/shard_map/ppermute | solution.py:110
  17.2 18.2 %copy-start.14 = (bf16[2,2,128,256]{3,2,1,0:T(8,128)(2,1)}, bf16[2,2,128,256]{3,2,1,0:T(8,128)(2,1)S(1)}, u32[]{:S(2)}) copy-start(bf16[2,2,128,256]{3,2,1,0:T(8,128)(2,1)S(1)} %constant_dynamic-slice_fusion.2) | copy-start | bytes 786436
  17.3 10.1 %copy-start.17 = (bf16[256,1,128]{2,0,1:T(8,128)(2,1)}, bf16[256,1,128]{2,0,1:T(8,128)(2,1)S(1)}, u32[]{:S(2)}) copy-start(bf16[256,1,128]{2,0,1:T(8,128)(2,1)S(1)} %collective-permute-done.5) | copy-start | bytes 196612
  38.1 26.0 %collective-permute-start.4 = (bf16[256,8,128]{0,2,1:T(8,128)(2,1)S(1)}, bf16[256,8,128]{0,2,1:T(8,128)(2,1)}, u32[]{:S(2)}, u32[]{:S(2)}) collective-permute-start(bf16[256,8,128]{0,2,1:T(8,128)(2,1)S(1)} %get-tuple-element.40), channel_id=1, source_target_pairs={{0,16},{16,0},{1,17},{17,1},{2,18},{18,2},{3,19},{19,3},{4,20},{20... | collective-permute-start | bytes 1572872 | tf_op jit(solution)/shard_map/ppermute | solution.py:110
  41.2 22.0 %collective-permute-start.3 = (bf16[256,1,128]{0,2,1:T(8,128)(2,1)}, bf16[256,1,128]{0,2,1:T(8,128)(2,1)}, u32[]{:S(2)}, u32[]{:S(2)}) collective-permute-start(bf16[256,1,128]{0,2,1:T(8,128)(2,1)} %get-tuple-element.36), channel_id=1, source_target_pairs={{0,17},{1,18},{2,19},{3,20},{4,21},{5,22},{6,23},{7,24},{8,25},{9,... | collective-permute-start | bytes 196616 | tf_op jit(solution)/shard_map/ppermute | solution.py:167
  43.4 9.5 %collective-permute-start.1 = (bf16[256,1,128]{0,2,1:T(8,128)(2,1)}, bf16[256,1,128]{0,2,1:T(8,128)(2,1)S(1)}, u32[]{:S(2)}, u32[]{:S(2)}) collective-permute-start(bf16[256,1,128]{0,2,1:T(8,128)(2,1)} %get-tuple-element.36), channel_id=1, source_target_pairs={{0,1},{1,2},{2,3},{3,4},{4,5},{5,6},{6,7},{7,8},{8,9},{9,10},{10,1... | collective-permute-start | bytes 196616 | tf_op jit(solution)/shard_map/ppermute | solution.py:167
  45.7 18.3 %collective-permute-start.7 = (bf16[256,1,128]{0,2,1:T(8,128)(2,1)}, bf16[256,1,128]{0,2,1:T(8,128)(2,1)}, u32[]{:S(2)}, u32[]{:S(2)}) collective-permute-start(bf16[256,1,128]{0,2,1:T(8,128)(2,1)} %get-tuple-element.37), channel_id=1, source_target_pairs={{1,16},{2,17},{3,18},{4,19},{5,20},{6,21},{7,22},{8,23},{9,24},{10... | collective-permute-start | bytes 196616 | tf_op jit(solution)/shard_map/ppermute | solution.py:168
  47.0 6.0 %collective-permute-start.2 = (bf16[256,1,128]{0,2,1:T(8,128)(2,1)}, bf16[256,1,128]{0,2,1:T(8,128)(2,1)S(1)}, u32[]{:S(2)}, u32[]{:S(2)}) collective-permute-start(bf16[256,1,128]{0,2,1:T(8,128)(2,1)} %get-tuple-element.37), channel_id=1, source_target_pairs={{1,0},{2,1},{3,2},{4,3},{5,4},{6,5},{7,6},{8,7},{9,8},{10,9},{11,1... | collective-permute-start | bytes 196616 | tf_op jit(solution)/shard_map/ppermute | solution.py:168
  57.0 21.1 %collective-permute-start.8 = (bf16[9,2,2,32,256]{4,3,2,1,0:T(8,128)(2,1)S(1)}, bf16[9,2,2,32,256]{4,3,2,1,0:T(8,128)(2,1)S(1)}, u32[]{:S(2)}, u32[]{:S(2)}) collective-permute-start(bf16[9,2,2,32,256]{4,3,2,1,0:T(8,128)(2,1)S(1)} %fusion.28), channel_id=1, source_target_pairs={{0,1},{1,0},{2,3},{3,2},{4,5},{5,4},{6,7},{7,6},{8,9},{9,8},{10,11... | collective-permute-start | bytes 1769480 | tf_op jit(solution)/shard_map/ppermute | solution.py:110
  71.5 20.3 %collective-permute-start.15 = (bf16[256,8,128]{0,2,1:T(8,128)(2,1)S(1)}, bf16[256,8,128]{0,2,1:T(8,128)(2,1)S(1)}, u32[]{:S(2)}, u32[]{:S(2)}) collective-permute-start(bf16[256,8,128]{0,2,1:T(8,128)(2,1)S(1)} %copy-done.21), channel_id=1, source_target_pairs={{0,16},{16,0},{1,17},{17,1},{2,18},{18,2},{3,19},{19,3},{4,20},{20... | collective-permute-start | bytes 1572872 | tf_op jit(solution)/shard_map/ppermute | solution.py:110
  72.2 42.5 %collective-permute-start.21 = (bf16[2,2,128,256]{3,2,1,0:T(8,128)(2,1)S(1)}, bf16[2,2,128,256]{3,2,1,0:T(8,128)(2,1)S(1)}, u32[]{:S(2)}, u32[]{:S(2)}) collective-permute-start(bf16[2,2,128,256]{3,2,1,0:T(8,128)(2,1)S(1)} %copy-done.15), channel_id=1, source_target_pairs={{0,16},{16,0},{1,17},{17,1},{2,18},{18,2},{3,19},{19,3},{4,20},{20... | collective-permute-start | bytes 786440 | tf_op jit(solution)/shard_map/ppermute | solution.py:110
  75.2 20.0 %collective-permute-start.11 = (bf16[9,2,2,32,256]{4,3,0,2,1:T(8,128)(2,1)S(1)}, bf16[9,2,2,32,256]{4,3,0,2,1:T(8,128)(2,1)S(1)}, u32[]{:S(2)}, u32[]{:S(2)}) collective-permute-start(bf16[9,2,2,32,256]{4,3,0,2,1:T(8,128)(2,1)S(1)} %fusion.29), channel_id=1, source_target_pairs={{0,1},{1,0},{2,3},{3,2},{4,5},{5,4},{6,7},{7,6},{8,9},{9,8},{10,11... | collective-permute-start | bytes 1769480 | tf_op jit(solution)/shard_map/ppermute | solution.py:110
  78.4 10.5 %collective-permute-start.9 = (bf16[9,2,32,256]{3,2,1,0:T(8,128)(2,1)S(1)}, bf16[9,2,32,256]{3,2,1,0:T(8,128)(2,1)S(1)}, u32[]{:S(2)}, u32[]{:S(2)}) collective-permute-start(bf16[9,2,32,256]{3,2,1,0:T(8,128)(2,1)S(1)} %fusion.108), channel_id=1, source_target_pairs={{0,2},{1,3},{2,0},{3,1},{4,6},{5,7},{6,4},{7,5},{8,10},{9,11},{10,... | collective-permute-start | bytes 884744 | tf_op jit(solution)/shard_map/ppermute | solution.py:110
  81.2 10.6 %copy-start.8 = (f32[256,8,128]{0,2,1:T(8,128)S(1)}, f32[256,8,128]{0,2,1:T(8,128)}, u32[]{:S(2)}) copy-start(f32[256,8,128]{0,2,1:T(8,128)} %get-tuple-element.41) | copy-start | bytes 3145732
  81.9 9.9 %copy-start.3 = (bf16[256,8,128]{2,0,1:T(8,128)(2,1)S(1)}, bf16[256,8,128]{2,0,1:T(8,128)(2,1)}, u32[]{:S(2)}) copy-start(bf16[256,8,128]{2,0,1:T(8,128)(2,1)} %copy-done.2) | copy-start | bytes 1572868
  81.9 9.9 %copy-start.5 = (f32[256,8,128]{0,2,1:T(8,128)S(1)}, f32[256,8,128]{0,2,1:T(8,128)}, u32[]{:S(2)}) copy-start(f32[256,8,128]{0,2,1:T(8,128)} %convolution_add_fusion.1) | copy-start | bytes 3145732
  81.9 9.9 %copy-start.7 = (f32[256,8,128]{0,2,1:T(8,128)S(1)}, f32[256,8,128]{0,2,1:T(8,128)}, u32[]{:S(2)}) copy-start(f32[256,8,128]{0,2,1:T(8,128)} %fusion.73) | copy-start | bytes 3145732
  89.0 21.4 %copy-start.9 = (f32[9,2,32,256]{3,2,1,0:T(8,128)}, f32[9,2,32,256]{3,2,1,0:T(8,128)S(1)}, u32[]{:S(2)}) copy-start(f32[9,2,32,256]{3,2,1,0:T(8,128)S(1)} %bitcast_add_fusion.2) | copy-start | bytes 1769476
  89.0 20.2 %collective-permute-start.10 = (bf16[9,32,256]{2,1,0:T(8,128)(2,1)S(1)}, bf16[9,32,256]{2,1,0:T(8,128)(2,1)S(1)}, u32[]{:S(2)}, u32[]{:S(2)}) collective-permute-start(bf16[9,32,256]{2,1,0:T(8,128)(2,1)S(1)} %fusion.117), channel_id=1, source_target_pairs={{0,4},{1,5},{2,6},{3,7},{4,0},{5,1},{6,2},{7,3},{8,12},{9,13},{10,... | collective-permute-start | bytes 442376 | tf_op jit(solution)/shard_map/ppermute | solution.py:110
  92.7 21.2 %collective-permute-start.19 = (bf16[256,8,128]{0,2,1:T(8,128)(2,1)S(1)}, bf16[256,8,128]{0,2,1:T(8,128)(2,1)S(1)}, u32[]{:S(2)}, u32[]{:S(2)}) collective-permute-start(bf16[256,8,128]{0,2,1:T(8,128)(2,1)S(1)} %fusion.18), channel_id=1, source_target_pairs={{0,16},{16,0},{1,17},{17,1},{2,18},{18,2},{3,19},{19,3},{4,20},{20... | collective-permute-start | bytes 1572872 | tf_op jit(solution)/shard_map/ppermute | solution.py:110
  94.3 1.6 %collective-permute-start.16 = (bf16[8,2,2,16,256]{4,3,2,1,0:T(8,128)(2,1)S(1)}, bf16[8,2,2,16,256]{4,3,2,1,0:T(8,128)(2,1)S(1)}, u32[]{:S(2)}, u32[]{:S(2)}) collective-permute-start(bf16[8,2,2,16,256]{4,3,2,1,0:T(8,128)(2,1)S(1)} %fusion.110), channel_id=1, source_target_pairs={{0,1},{1,0},{2,3},{3,2},{4,5},{5,4},{6,7},{7,6},{8,9},{9,8},{10,11... | collective-permute-start | bytes 786440 | tf_op jit(solution)/shard_map/ppermute | solution.py:110
  95.5 9.1 %collective-permute-start.12 = (bf16[9,2,32,256]{3,2,0,1:T(8,128)(2,1)S(1)}, bf16[9,2,32,256]{3,2,0,1:T(8,128)(2,1)S(1)}, u32[]{:S(2)}, u32[]{:S(2)}) collective-permute-start(bf16[9,2,32,256]{3,2,0,1:T(8,128)(2,1)S(1)} %fusion.109), channel_id=1, source_target_pairs={{0,4},{1,5},{2,6},{3,7},{4,0},{5,1},{6,2},{7,3},{8,12},{9,13},{10,... | collective-permute-start | bytes 884744 | tf_op jit(solution)/shard_map/ppermute | solution.py:110
  96.0 8.7 %collective-permute-start.17 = (bf16[8,2,16,256]{3,2,1,0:T(8,128)(2,1)S(1)}, bf16[8,2,16,256]{3,2,1,0:T(8,128)(2,1)S(1)}, u32[]{:S(2)}, u32[]{:S(2)}) collective-permute-start(bf16[8,2,16,256]{3,2,1,0:T(8,128)(2,1)S(1)} %fusion.119), channel_id=1, source_target_pairs={{0,2},{1,3},{2,0},{3,1},{4,6},{5,7},{6,4},{7,5},{8,10},{9,11},{10,... | collective-permute-start | bytes 393224 | tf_op jit(solution)/shard_map/ppermute | solution.py:110
  104.7 10.0 %copy-start.10 = (f32[9,2,32,256]{3,2,0,1:T(8,128)}, f32[9,2,32,256]{3,2,0,1:T(8,128)S(1)}, u32[]{:S(2)}) copy-start(f32[9,2,32,256]{3,2,0,1:T(8,128)S(1)} %bitcast_add_fusion.1) | copy-start | bytes 1769476
  104.8 4.3 %collective-permute-start.18 = (bf16[8,16,256]{2,1,0:T(8,128)(2,1)S(1)}, bf16[8,16,256]{2,1,0:T(8,128)(2,1)S(1)}, u32[]{:S(2)}, u32[]{:S(2)}) collective-permute-start(bf16[8,16,256]{2,1,0:T(8,128)(2,1)S(1)} %fusion.120), channel_id=1, source_target_pairs={{0,4},{1,5},{2,6},{3,7},{4,0},{5,1},{6,2},{7,3},{8,12},{9,13},{10,... | collective-permute-start | bytes 196616 | tf_op jit(solution)/shard_map/ppermute | solution.py:110
  105.1 5.2 %collective-permute-start.13 = (bf16[9,32,256]{2,1,0:T(8,128)(2,1)S(1)}, bf16[9,32,256]{2,1,0:T(8,128)(2,1)S(1)}, u32[]{:S(2)}, u32[]{:S(2)}) collective-permute-start(bf16[9,32,256]{2,1,0:T(8,128)(2,1)S(1)} %fusion.118), channel_id=1, source_target_pairs={{0,2},{1,3},{2,0},{3,1},{4,6},{5,7},{6,4},{7,5},{8,10},{9,11},{10,... | collective-permute-start | bytes 442376 | tf_op jit(solution)/shard_map/ppermute | solution.py:110
  111.1 11.5 %collective-permute-start.14 = (bf16[9,32,256]{2,1,0:T(8,128)(2,1)}, bf16[9,32,256]{2,1,0:T(8,128)(2,1)}, u32[]{:S(2)}, u32[]{:S(2)}) collective-permute-start(bf16[9,32,256]{2,1,0:T(8,128)(2,1)} %select_convert_fusion), channel_id=1, source_target_pairs={{0,8},{1,9},{2,10},{3,11},{4,12},{5,13},{6,14},{7,15},{8,0},{9,1},... | collective-permute-start | bytes 442376 | tf_op jit(solution)/shard_map/ppermute | solution.py:110
  114.5 6.6 %collective-permute-start.20 = (bf16[4,16,256]{2,1,0:T(8,128)(2,1)}, bf16[4,16,256]{2,1,0:T(8,128)(2,1)}, u32[]{:S(2)}, u32[]{:S(2)}) collective-permute-start(bf16[4,16,256]{2,1,0:T(8,128)(2,1)} %select_convert_fusion.1), channel_id=1, source_target_pairs={{0,8},{1,9},{2,10},{3,11},{4,12},{5,13},{6,14},{7,15},{8,0},{9,1},... | collective-permute-start | bytes 98312 | tf_op jit(solution)/shard_map/ppermute | solution.py:110
  (12 other events, 38.0 us)
